TPU v7x, 768 devices: a whole 4x8x12 slice. The times are simulated.
768 devices in a mesh: lat: 48 (over z, x_hi, core), lon: 16 (over x_lo, y).
Axes of the slice: x: 4 (x_hi: 2, x_lo: 2; x = x_hi * 2 + x_lo), y: 8, z: 12, core: 2. Of those that a mesh axis runs over, the one named last changes fastest.
Arguments:
- elem_codes: int32 [768, 128, 256], P('lat', 'lon'), may hold values from 32 to 207, as said below
- block_exps: int32 [768, 128, 8], P('lat', 'lon'), may hold values from -2 to 1
- up_kernel: bfloat16 [4, 4, 256, 128], replicated, may hold values from -0.1875 to 0.1875
- up_bias: float32 [128], replicated, may hold values from -3 to 3
- mix_kernel: bfloat16 [3, 3, 128, 128], replicated, may hold values from -0.1875 to 0.1875
- cotangent: bfloat16 [1536, 256, 128], P('lat', 'lon'), may hold values from -6 to 6
Outputs:
- section_out: bfloat16 [1536, 256, 128], P('lat', 'lon')
- input_grad: float32 [768, 128, 256], P('lat', 'lon')
- up_grad: float32 [4, 4, 256, 128], P(None, None, 'lon')
- mix_grad: float32 [3, 3, 128, 128], P(None, None, 'lon')
Inputs may be any that keep to these rules, and one draw needn't show every extreme that they name: `elem_codes`: every code has a sign bit of weight 128, a four-bit exponent field from 4 to 9 and a three-bit mantissa.
All inputs are finite; a program needn't handle non-finite values.
Results may differ from a plain program's by a relative error of at most 0.012.
Values may be sent and summed in bfloat16 or wider, within the bound.
A program may use at most 32 MiB of HBM per device.

v0:
```python
import math

import jax
import jax.numpy as jnp
from jax import lax
from jax.sharding import PartitionSpec as P

CIN = 256
COUT = 128
BLOCK = 32


row_taps = (((1, 0), (3, -1)), ((0, 1), (2, 0)))


def padded_2(array, sides, width, wrap):
    for axis, dim in sides:
        size, length = (lax.axis_size(axis), array.shape[dim])
        up = [(i, (i + 1) % size) for i in range(size if wrap else size - 1)]
        down = [(j, i) for i, j in up]
        last = lax.slice_in_dim(array, length - width, length, axis=dim)
        leading = lax.slice_in_dim(array, 0, width, axis=dim)
        before = lax.ppermute(last, axis, up)
        after = lax.ppermute(leading, axis, down)
        array = jnp.concatenate([before, array, after], axis=dim)
    return array


def decode(elem_codes, block_exps):
    sign_bit = elem_codes // 128
    exponent = elem_codes // 8 % 16
    mantissa = elem_codes % 8
    magnitude = jnp.exp2((exponent - 7).astype(jnp.float32)) * (
        1.0 + mantissa.astype(jnp.float32) / 8.0
    )
    signed = jnp.where(sign_bit == 1, -magnitude, magnitude)
    factor = jnp.repeat(jnp.exp2(block_exps.astype(jnp.float32)), BLOCK, axis=2)
    return (signed * factor).astype(jnp.bfloat16)


def extend(field, margin):
    widened = padded_2(field, (("lon", 1),), margin, True)
    return padded_2(widened, (("lat", 0),), margin, False)


def slope(pre_act):
    plain = pre_act.astype(jnp.float32)
    sigmoid_v = jax.nn.sigmoid(plain)
    return sigmoid_v * (1.0 + plain * (1.0 - sigmoid_v))


def upsample(padded, up_kernel, row_count, col_count):
    halves = []
    for row_par in range(2):
        lane_list = []
        for col_par in range(2):
            pieces = []
            kernels = []
            for row_tap, row_off in row_taps[row_par]:
                for col_tap, col_off in row_taps[col_par]:
                    pieces.append(
                        padded[
                            1 + row_off : 1 + row_off + row_count,
                            1 + col_off : 1 + col_off + col_count,
                        ]
                    )
                    kernels.append(up_kernel[row_tap, col_tap])
            stacked = jnp.concatenate(pieces, axis=2)
            kernel = jnp.concatenate(kernels, axis=0)
            lane_list.append(
                jnp.einsum("rck,kn->rcn", stacked, kernel, preferred_element_type=jnp.float32)
            )
        halves.append(jnp.stack(lane_list, axis=2))
    merged = jnp.stack(halves, axis=1)
    return merged.reshape(2 * row_count, 2 * col_count, merged.shape[-1])


def neighbours(padded, row_count, col_count, flipped):
    pieces = []
    for row_tap in range(3):
        for col_tap in range(3):
            row_at = 2 - row_tap if flipped else row_tap
            col_at = 2 - col_tap if flipped else col_tap
            pieces.append(padded[row_at : row_at + row_count, col_at : col_at + col_count])
    return jnp.concatenate(pieces, axis=2)


def strided(padded, row_count, col_count):
    pieces = []
    for row_tap in range(4):
        for col_tap in range(4):
            pieces.append(
                padded[row_tap : row_tap + 2 * row_count : 2, col_tap : col_tap + 2 * col_count : 2]
            )
    return jnp.concatenate(pieces, axis=2)


def shards(elem_codes, block_exps, up_kernel, up_bias, mix_kernel, cotangent):
    inputs = decode(elem_codes, block_exps)
    in_rows, in_cols = (inputs.shape[0], inputs.shape[1])
    out_rows, out_cols = (2 * in_rows, 2 * in_cols)
    lat_count = lax.axis_size("lat")
    lon_count = lax.axis_size("lon")
    back_mix = mix_kernel.transpose(0, 1, 3, 2).reshape(9 * COUT, COUT)
    padded_in = extend(inputs, 1)
    raw = upsample(padded_in, up_kernel, in_rows, in_cols)
    pre_act = (raw + up_bias).astype(jnp.bfloat16)
    act_pad = extend(jax.nn.silu(pre_act.astype(jnp.float32)).astype(jnp.bfloat16), 1)
    grad_pad = extend(cotangent, 1)
    act_grad = jnp.einsum(
        "rck,kn->rcn",
        neighbours(grad_pad, out_rows, out_cols, True),
        back_mix,
        preferred_element_type=jnp.float32,
    )
    pre_grad_pad = extend((act_grad * slope(pre_act)).astype(jnp.bfloat16), 1)
    patches = neighbours(act_pad, out_rows, out_cols, False)
    mix_flat = mix_kernel.reshape(9 * COUT, COUT)
    section_out = jnp.einsum(
        "rck,kn->rcn", patches, mix_flat, preferred_element_type=jnp.float32
    ).astype(jnp.bfloat16)
    grad_scale = 1.0 / math.sqrt(out_rows * lat_count * out_cols * lon_count)
    mix_grad = (
        jnp.einsum("rck,rcn->kn", patches, cotangent, preferred_element_type=jnp.float32).reshape(
            3, 3, COUT, COUT
        )
        * grad_scale
    )
    grad_patches = strided(pre_grad_pad, in_rows, in_cols)
    back_up = up_kernel.transpose(0, 1, 3, 2).reshape(16 * COUT, CIN)
    input_grad = jnp.einsum(
        "rck,kn->rcn", grad_patches, back_up, preferred_element_type=jnp.float32
    )
    up_flat = jnp.einsum("rcm,rck->mk", inputs, grad_patches, preferred_element_type=jnp.float32)
    up_grad = up_flat.reshape(CIN, 4, 4, COUT).transpose(1, 2, 0, 3) * grad_scale
    summed = lax.psum((up_grad, mix_grad), ("lat", "lon"))
    lon_index = lax.axis_index("lon")
    up_span = CIN // lon_count
    mix_span = COUT // lon_count
    up_part = lax.dynamic_slice_in_dim(summed[0], lon_index * up_span, up_span, 2)
    mix_part = lax.dynamic_slice_in_dim(summed[1], lon_index * mix_span, mix_span, 2)
    return (section_out, input_grad, up_part, mix_part)


def solution(mesh):
    placed = (P("lat", "lon", None), P("lat", "lon", None), P(), P(), P(), P("lat", "lon", None))
    return jax.shard_map(
        shards,
        mesh=mesh,
        in_specs=placed,
        out_specs=(
            P("lat", "lon", None),
            P("lat", "lon", None),
            P(None, None, "lon", None),
            P(None, None, "lon", None),
        ),
        check_vma=False,
    )
```

profile of v0, /device:TPU:1, one launch (start us, length us, event | category | flops | bytes accessed | tf_op | source)
XLA Modules:
  0.0 600.6 jit_solution(8237275640464608861)
XLA Ops:
  7.2 0.9 multiply_exponential_fusion
  8.9 4.2 collective-permute-start
  13.1 4.7 collective-permute-start.1
  17.9 3.4 collective-permute-start.9
  21.3 1.9 collective-permute-start.8
  23.6 5.8 collective-permute-start.2
  29.4 7.7 %collective-permute-start.3 = (bf16[1,10,256]{2,1,0:T(8,128)(2,1)S(1)}, bf16[1,10,256]{2,1,0:T(8,128)(2,1)S(1)}, u32[]{:S(2)}, u32[]{:S(2)}) collective-permute-start(bf16[1,10,256]{2,1,0:T(8,128)(2,1)S(1)} %get-tuple-element.47), channel_id=1, source_target_pairs={{16,0},{32,16},{48,32},{64,48},{80,64},{96,80},{112,96},{128,112},... | collective-permute-start | bytes 15368 | tf_op jit(solution)/shard_map/ppermute | solution.py:24
  37.1 1.9 collective-permute-start.11
  39.0 2.4 collective-permute-start.10
  41.5 4.0 collective-permute-done.10
  48.4 3.8 collective-permute-start.13
  52.1 1.9 collective-permute-start.12
  54.4 5.5 collective-permute-start.5
  59.9 1.9 collective-permute-start.4
  62.0 1.9 collective-permute-start.15
  63.9 5.1 collective-permute-start.14
  70.2 1.9 collective-permute-start.7
  72.1 5.1 collective-permute-start.6
  81.5 0.7 slice.314
  82.3 0.7 slice.315
  83.8 1.1 copy-done.2
  85.2 0.8 copy-done.6
  85.9 1.8 fusion
  87.8 2.7 mul.54
  90.5 2.0 copy.30
  92.5 1.4 fusion.1
  94.4 0.7 copy-done.4
  95.1 2.1 convolution_convert_fusion
  97.2 1.0 fusion.91
  98.2 492.6 %all-reduce.3.cloned.1.call-done = (f32[4,4,256,128]{3,2,1,0:T(8,128)}, f32[3,3,128,128]{3,2,1,0:T(8,128)}) async-done(((f32[4,4,256,128]{3,2,1,0:T(8,128)}, f32[3,3,128,128]{3,2,1,0:T(8,128)}), (f32[4,4,256,128]{3,2,1,0:T(8,128)}, f32[3,3,128,128]{3,2,1,0:T(8,128)})) %all-reduce.3.cloned.1.call-update) | async-done | bytes 2686992 | tf_op jit(solution)/shard_map/psum | solution.py:136
  590.8 1.6 constant_dynamic-slice_fusion.1
  592.3 1.4 constant_dynamic-slice_fusion
  (114 shorter events, 11.3 us)
Async XLA Ops:
  7.2 1.4 copy-start.8
  7.2 10.7 %copy-start.1 = (bf16[32,16,128]{2,1,0:T(8,128)(2,1)S(1)}, bf16[32,16,128]{2,1,0:T(8,128)(2,1)}, u32[]{:S(2)}) copy-start(bf16[32,16,128]{2,1,0:T(8,128)(2,1)} %param.11) | copy-start | bytes 393220
  7.2 16.0 %copy-start = (bf16[4,4,256,128]{3,2,1,0:T(8,128)(2,1)S(1)}, bf16[4,4,256,128]{3,2,1,0:T(8,128)(2,1)}, u32[]{:S(2)}) copy-start(bf16[4,4,256,128]{3,2,1,0:T(8,128)(2,1)} %param.8) | copy-start | bytes 3145732
  7.2 583.6 %all-reduce.3.cloned.1.call-start = ((), (), s32[]{:S(2)}) async-start(), calls=%async_computation | async-start | bytes 5373952 | tf_op jit(solution)/shard_map/psum | solution.py:136
  8.9 14.4 %copy-start.5 = (bf16[3,3,128,128]{3,2,1,0:T(8,128)(2,1)S(1)}, bf16[3,3,128,128]{3,2,1,0:T(8,128)(2,1)}, u32[]{:S(2)}) copy-start(bf16[3,3,128,128]{3,2,1,0:T(8,128)(2,1)} %param.10) | copy-start | bytes 884740
  8.9 14.6 %collective-permute-start = (bf16[16,1,256]{2,1,0:T(2,128)(2,1)S(1)}, bf16[16,1,256]{2,1,0:T(2,128)(2,1)S(1)}, u32[]{:S(2)}, u32[]{:S(2)}) collective-permute-start(bf16[16,1,256]{2,1,0:T(2,128)(2,1)S(1)} %get-tuple-element.50), channel_id=1, source_target_pairs={{0,1},{1,2},{2,3},{3,4},{4,5},{5,6},{6,7},{7,8},{8,9},{9,10},{10,1... | collective-permute-start | bytes 24584 | tf_op jit(solution)/shard_map/ppermute | solution.py:23
  13.1 10.4 %collective-permute-start.1 = (bf16[16,1,256]{2,1,0:T(2,128)(2,1)S(1)}, bf16[16,1,256]{2,1,0:T(2,128)(2,1)S(1)}, u32[]{:S(2)}, u32[]{:S(2)}) collective-permute-start(bf16[16,1,256]{2,1,0:T(2,128)(2,1)S(1)} %get-tuple-element.51), channel_id=1, source_target_pairs={{1,0},{2,1},{3,2},{4,3},{5,4},{6,5},{7,6},{8,7},{9,8},{10,9},{11,1... | collective-permute-start | bytes 24584 | tf_op jit(solution)/shard_map/ppermute | solution.py:24
  17.9 19.1 %collective-permute-start.9 = (bf16[32,1,128]{2,1,0:T(2,128)(2,1)S(1)}, bf16[32,1,128]{2,1,0:T(2,128)(2,1)S(1)}, u32[]{:S(2)}, u32[]{:S(2)}) collective-permute-start(bf16[32,1,128]{2,1,0:T(2,128)(2,1)S(1)} %get-tuple-element.41), channel_id=1, source_target_pairs={{1,0},{2,1},{3,2},{4,3},{5,4},{6,5},{7,6},{8,7},{9,8},{10,9},{11,1... | collective-permute-start | bytes 24584 | tf_op jit(solution)/shard_map/ppermute | solution.py:24
  21.3 15.8 %collective-permute-start.8 = (bf16[32,1,128]{2,1,0:T(2,128)(2,1)S(1)}, bf16[32,1,128]{2,1,0:T(2,128)(2,1)S(1)}, u32[]{:S(2)}, u32[]{:S(2)}) collective-permute-start(bf16[32,1,128]{2,1,0:T(2,128)(2,1)S(1)} %get-tuple-element.40), channel_id=1, source_target_pairs={{0,1},{1,2},{2,3},{3,4},{4,5},{5,6},{6,7},{7,8},{8,9},{9,10},{10,1... | collective-permute-start | bytes 24584 | tf_op jit(solution)/shard_map/ppermute | solution.py:23
  23.6 22.6 %collective-permute-start.2 = (bf16[1,10,256]{2,1,0:T(8,128)(2,1)S(1)}, bf16[1,10,256]{2,1,0:T(8,128)(2,1)S(1)}, u32[]{:S(2)}, u32[]{:S(2)}) collective-permute-start(bf16[1,10,256]{2,1,0:T(8,128)(2,1)S(1)} %get-tuple-element.46), channel_id=1, source_target_pairs={{0,16},{16,32},{32,48},{48,64},{64,80},{80,96},{96,112},{112,128},... | collective-permute-start | bytes 15368 | tf_op jit(solution)/shard_map/ppermute | solution.py:23
  29.4 16.8 %collective-permute-start.3 = (bf16[1,10,256]{2,1,0:T(8,128)(2,1)S(1)}, bf16[1,10,256]{2,1,0:T(8,128)(2,1)S(1)}, u32[]{:S(2)}, u32[]{:S(2)}) collective-permute-start(bf16[1,10,256]{2,1,0:T(8,128)(2,1)S(1)} %get-tuple-element.47), channel_id=1, source_target_pairs={{16,0},{32,16},{48,32},{64,48},{80,64},{96,80},{112,96},{128,112},... | collective-permute-start | bytes 15368 | tf_op jit(solution)/shard_map/ppermute | solution.py:24
  37.1 4.4 collective-permute-start.11
  39.0 6.5 %collective-permute-start.10 = (bf16[1,18,128]{2,1,0:T(8,128)(2,1)S(1)}, bf16[1,18,128]{2,1,0:T(8,128)(2,1)S(1)}, u32[]{:S(2)}, u32[]{:S(2)}) collective-permute-start(bf16[1,18,128]{2,1,0:T(8,128)(2,1)S(1)} %get-tuple-element.27), channel_id=1, source_target_pairs={{16,0},{32,16},{48,32},{64,48},{80,64},{96,80},{112,96},{128,112},... | collective-permute-start | bytes 13832 | tf_op jit(solution)/shard_map/ppermute | solution.py:24
  47.1 0.7 copy-start.9
  48.4 13.5 %collective-permute-start.13 = (bf16[32,1,128]{2,1,0:T(2,128)(2,1)S(1)}, bf16[32,1,128]{2,1,0:T(2,128)(2,1)S(1)}, u32[]{:S(2)}, u32[]{:S(2)}) collective-permute-start(bf16[32,1,128]{2,1,0:T(2,128)(2,1)S(1)} %get-tuple-element.39), channel_id=1, source_target_pairs={{1,0},{2,1},{3,2},{4,3},{5,4},{6,5},{7,6},{8,7},{9,8},{10,9},{11,1... | collective-permute-start | bytes 24584 | tf_op jit(solution)/shard_map/ppermute | solution.py:24
  52.1 9.7 %collective-permute-start.12 = (bf16[32,1,128]{2,1,0:T(2,128)(2,1)S(1)}, bf16[32,1,128]{2,1,0:T(2,128)(2,1)S(1)}, u32[]{:S(2)}, u32[]{:S(2)}) collective-permute-start(bf16[32,1,128]{2,1,0:T(2,128)(2,1)S(1)} %get-tuple-element.38), channel_id=1, source_target_pairs={{0,1},{1,2},{2,3},{3,4},{4,5},{5,6},{6,7},{7,8},{8,9},{9,10},{10,1... | collective-permute-start | bytes 24584 | tf_op jit(solution)/shard_map/ppermute | solution.py:23
  54.4 14.6 %collective-permute-start.5 = (bf16[32,1,128]{2,1,0:T(2,128)(2,1)S(1)}, bf16[32,1,128]{2,1,0:T(2,128)(2,1)S(1)}, u32[]{:S(2)}, u32[]{:S(2)}) collective-permute-start(bf16[32,1,128]{2,1,0:T(2,128)(2,1)S(1)} %get-tuple-element.43), channel_id=1, source_target_pairs={{1,0},{2,1},{3,2},{4,3},{5,4},{6,5},{7,6},{8,7},{9,8},{10,9},{11,1... | collective-permute-start | bytes 24584 | tf_op jit(solution)/shard_map/ppermute | solution.py:24
  59.9 9.2 %collective-permute-start.4 = (bf16[32,1,128]{2,1,0:T(2,128)(2,1)S(1)}, bf16[32,1,128]{2,1,0:T(2,128)(2,1)S(1)}, u32[]{:S(2)}, u32[]{:S(2)}) collective-permute-start(bf16[32,1,128]{2,1,0:T(2,128)(2,1)S(1)} %get-tuple-element.42), channel_id=1, source_target_pairs={{0,1},{1,2},{2,3},{3,4},{4,5},{5,6},{6,7},{7,8},{8,9},{9,10},{10,1... | collective-permute-start | bytes 24584 | tf_op jit(solution)/shard_map/ppermute | solution.py:23
  62.0 15.3 %collective-permute-start.15 = (bf16[1,18,128]{2,1,0:T(8,128)(2,1)S(1)}, bf16[1,18,128]{2,1,0:T(8,128)(2,1)S(1)}, u32[]{:S(2)}, u32[]{:S(2)}) collective-permute-start(bf16[1,18,128]{2,1,0:T(8,128)(2,1)S(1)} %get-tuple-element.23), channel_id=1, source_target_pairs={{16,0},{32,16},{48,32},{64,48},{80,64},{96,80},{112,96},{128,112},... | collective-permute-start | bytes 13832 | tf_op jit(solution)/shard_map/ppermute | solution.py:24
  63.9 13.4 %collective-permute-start.14 = (bf16[1,18,128]{2,1,0:T(8,128)(2,1)S(1)}, bf16[1,18,128]{2,1,0:T(8,128)(2,1)S(1)}, u32[]{:S(2)}, u32[]{:S(2)}) collective-permute-start(bf16[1,18,128]{2,1,0:T(8,128)(2,1)S(1)} %get-tuple-element.22), channel_id=1, source_target_pairs={{0,16},{16,32},{32,48},{48,64},{64,80},{80,96},{96,112},{112,128},... | collective-permute-start | bytes 13832 | tf_op jit(solution)/shard_map/ppermute | solution.py:23
  70.2 12.8 %collective-permute-start.7 = (bf16[1,18,128]{2,1,0:T(8,128)(2,1)S(1)}, bf16[1,18,128]{2,1,0:T(8,128)(2,1)S(1)}, u32[]{:S(2)}, u32[]{:S(2)}) collective-permute-start(bf16[1,18,128]{2,1,0:T(8,128)(2,1)S(1)} %get-tuple-element.30), channel_id=1, source_target_pairs={{16,0},{32,16},{48,32},{64,48},{80,64},{96,80},{112,96},{128,112},... | collective-permute-start | bytes 13832 | tf_op jit(solution)/shard_map/ppermute | solution.py:24
  72.1 10.9 %collective-permute-start.6 = (bf16[1,18,128]{2,1,0:T(8,128)(2,1)S(1)}, bf16[1,18,128]{2,1,0:T(8,128)(2,1)S(1)}, u32[]{:S(2)}, u32[]{:S(2)}) collective-permute-start(bf16[1,18,128]{2,1,0:T(8,128)(2,1)S(1)} %get-tuple-element.31), channel_id=1, source_target_pairs={{0,16},{16,32},{32,48},{48,64},{64,80},{80,96},{96,112},{112,128},... | collective-permute-start | bytes 13832 | tf_op jit(solution)/shard_map/ppermute | solution.py:23
  83.8 1.1 copy-start.2
  85.2 0.8 copy-start.6
  90.5 2.0 copy-start.3
  93.8 1.3 copy-start.4
  94.4 2.8 copy-start.7
Sparse Core Ops, SparseCore 0:
  94.0 496.7 all-reduce.2
where the time goes:
time: 601 us
  waiting for transfers between devices  497 us (83%)
  starting transfers between devices  59.2 us (10%)
  local copies, waits for them, and re-layouts  19.8 us (3%)
  between operations  14.8 us (2%)
  matrix products  7.65 us (1%)
    psum x1, waiting for transfers between devices, shards(): summed = lax.psum((up_grad, mix_grad), ('lat', 'lon'))  493 us
    ppermute x8, starting transfers between devices, padded_2(): after = lax.ppermute(leading, axis, down)  31.2 us
    ppermute x8, starting transfers between devices, padded_2(): before = lax.ppermute(last, axis, up)  27.9 us
  transfers between devices with their start and end apart: 17, of which 2 were waited for; matrix products, arithmetic and copies ran while one was open for 2% of the time, Pallas kernels for 0%

commit v1 on v0

v1 whole, which is shorter than its diff:
```python
import functools
import math

import jax
import jax.numpy as jnp
from jax import lax
from jax.experimental import pallas as pl
from jax.experimental.pallas import tpu as pltpu
from jax.sharding import PartitionSpec as P

CIN = 256
COUT = 128
ROWS = 16
COLS = 8
PITCH = 10
CELLS = ROWS * COLS
TALL = CIN // COUT + 4
FLAT = 192
OUTER = 176
INNER = ROWS * PITCH
PARTS = 3
SPAN = 2 * COUT
TILES = 4 * PARTS
LON_ALL = 16
MESH = pl.DeviceIdType.MESH
F32 = jnp.float32
BF16 = jnp.bfloat16


def power_bits(value, bits):
    total = jnp.where(value & 1 != 0, 2.0, 1.0)
    for bit in range(1, bits):
        total = total * jnp.where(value & (1 << bit) != 0, float(1 << (1 << bit)), 1.0)
    return total


def decode(codes, exps):
    sign = jnp.where(codes >= 128, -(2.0**-9), 2.0**-9)
    fraction = (8 + (codes & 7)).astype(F32) * 0.125
    signed = sign * power_bits((codes >> 3) & 15, 4) * fraction
    factor = power_bits(exps + 2, 2).astype(BF16)
    blocks = exps.shape[1]
    channel = lax.broadcasted_iota(jnp.int32, (blocks, CIN), 1)
    block = lax.broadcasted_iota(jnp.int32, (blocks, CIN), 0)
    spread = jnp.where(channel // (CIN // blocks) == block, 1.0, 0.0).astype(BF16)
    return signed * jnp.dot(factor, spread, preferred_element_type=F32)


def halo_partners(lat, lon, lat_count, lon_count):
    up, down = lax.rem(lat + lat_count - 1, lat_count), lax.rem(lat + 1, lat_count)
    left, right = lax.rem(lon + lon_count - 1, lon_count), lax.rem(lon + 1, lon_count)
    return up, down, left, right


def halo_fill(codes, exps, cot, grid, own, cot_wide, row_out, col_out, corner_out):
    decoded = decode(codes[...], exps[...])
    for i in range(CIN // COUT):
        own[i] = decoded[:, i * COUT : (i + 1) * COUT]
    cot_wide[...] = cot[...].astype(F32)
    for r in range(ROWS):
        for s in range(2):
            for t in range(2):
                own[2 + 2 * s + t, r * COLS : (r + 1) * COLS, :] = cot_wide[
                    pl.ds((2 * r + s) * 2 * COLS + t, COLS, stride=2), :
                ]
    for side, r in enumerate((ROWS - 1, 0)):
        for i in range(TALL // 2):
            row_out[side, i] = jnp.concatenate(
                [own[j, r * COLS : (r + 1) * COLS, :] for j in (2 * i, 2 * i + 1)], axis=0
            ).astype(BF16)
    for side, c in enumerate((COLS - 1, 0)):
        for i in range(TALL):
            col_out[side, i] = own[i, pl.ds(c, ROWS, stride=COLS), :].astype(BF16)
    for corner, (r, c) in enumerate(((ROWS - 1, COLS - 1), (ROWS - 1, 0), (0, COLS - 1), (0, 0))):
        cell = r * COLS + c
        corner_out[corner] = jnp.zeros((8, COUT), F32)
        for i in range(TALL):
            corner_out[corner, i : i + 1, :] = own[i, cell : cell + 1, :]
    for r in range(ROWS):
        at = (r + 1) * PITCH + 1
        for i in range(TALL):
            grid[i, at : at + COLS, :] = own[i, r * COLS : (r + 1) * COLS, :]
    tail = (ROWS + 2) * PITCH
    for i in range(TALL):
        grid[i, tail:FLAT, :] = jnp.zeros((FLAT - tail, COUT), F32)


def halo_copies(partners, lat, lon, row_out, col_out, corner_out, row_in, col_in, corner_in, send, recv):
    up, down, left, right = partners
    plan = [
        (row_out.at[0], row_in.at[0], down, lon),
        (row_out.at[1], row_in.at[1], up, lon),
        (col_out.at[0], col_in.at[0], lat, right),
        (col_out.at[1], col_in.at[1], lat, left),
        (corner_out.at[0], corner_in.at[0], down, right),
        (corner_out.at[1], corner_in.at[1], down, left),
        (corner_out.at[2], corner_in.at[2], up, right),
        (corner_out.at[3], corner_in.at[3], up, left),
    ]
    return [
        pltpu.make_async_remote_copy(
            src_ref=src,
            dst_ref=dst,
            send_sem=send.at[i],
            recv_sem=recv.at[i],
            device_id=(to_lat, to_lon),
            device_id_type=MESH,
        )
        for i, (src, dst, to_lat, to_lon) in enumerate(plan)
    ]


def halo_place(lat, lat_count, grid, row_in, col_in, corner_in):
    above = (lat > 0).astype(F32)
    below = (lat < lat_count - 1).astype(F32)
    for side, (r, keep) in enumerate(((0, above), (ROWS + 1, below))):
        at = r * PITCH + 1
        for i in range(TALL // 2):
            part = row_in[side, i].astype(F32) * keep
            grid[2 * i, at : at + COLS, :] = part[:COLS]
            grid[2 * i + 1, at : at + COLS, :] = part[COLS:]
    for side, c in enumerate((0, COLS + 1)):
        for i in range(TALL):
            grid[i, pl.ds(PITCH + c, ROWS, stride=PITCH), :] = col_in[side, i].astype(F32)
    places = ((0, 0, above), (0, COLS + 1, above), (ROWS + 1, 0, below), (ROWS + 1, COLS + 1, below))
    for corner, (r, c, keep) in enumerate(places):
        cell = r * PITCH + c
        for i in range(TALL):
            grid[i, cell : cell + 1, :] = corner_in[corner, i : i + 1, :] * keep


def halo_kernel(
    lat_count,
    lon_count,
    codes,
    exps,
    cot,
    grid,
    own,
    cot_wide,
    row_out,
    col_out,
    corner_out,
    row_in,
    col_in,
    corner_in,
    send,
    recv,
):
    lat, lon = lax.axis_index("lat"), lax.axis_index("lon")
    partners = halo_partners(lat, lon, lat_count, lon_count)
    up, down, left, right = partners
    barrier = pltpu.get_barrier_semaphore()
    for to_lat in (up, lat, down):
        for to_lon in (left, lon, right):
            if to_lat is lat and to_lon is lon:
                continue
            pl.semaphore_signal(barrier, inc=1, device_id=(to_lat, to_lon), device_id_type=MESH)
    halo_fill(codes, exps, cot, grid, own, cot_wide, row_out, col_out, corner_out)
    pl.semaphore_wait(barrier, 8)
    copies = halo_copies(
        partners, lat, lon, row_out, col_out, corner_out, row_in, col_in, corner_in, send, recv
    )
    for copy in copies:
        copy.start()
    for copy in copies:
        copy.wait()
    halo_place(lat, lat_count, grid, row_in, col_in, corner_in)


OFFSETS = ((0, 0), (0, 1), (1, 0), (1, 1))


def positions(ref, length, low):
    found = {}
    for dr, dc in OFFSETS:
        for pr in range(2):
            for pc in range(2):
                found[2 * dr + pr, 2 * dc + pc] = ref[
                    low + 2 * pr + pc, pl.ds(dr * PITCH + dc, length), :
                ].astype(BF16)
    return found


def window(ref, start, length, low, high):
    return jnp.concatenate([ref[i, pl.ds(start, length), :] for i in range(low, high)], axis=1)


def keep_wide(ref, value):
    for i in range(4):
        ref[i, :OUTER, :] = value[:, i * COUT : (i + 1) * COUT]
        ref[i, OUTER:, :] = jnp.zeros((FLAT - OUTER, COUT), F32)


def patches(found, flipped):
    stacked = []
    for s in range(2):
        for t in range(2):
            pieces = []
            for ky in range(3):
                for kx in range(3):
                    at = (s - ky + 2, t - kx + 2) if flipped else (s + ky, t + kx)
                    pieces.append(found[at])
            stacked.append(jnp.concatenate(pieces, axis=1))
    return jnp.concatenate(stacked, axis=0)


def beside(array, rows):
    return jnp.concatenate([array[i * rows : (i + 1) * rows] for i in range(4)], axis=1)


def inner_mask(lanes):
    cell = lax.broadcasted_iota(jnp.int32, (INNER, lanes), 0)
    return lax.rem(cell, PITCH) < COLS


def compute_kernel(
    lat_count, grid, up_kernel, bias, mix_kernel, section, input_grad, sums, act, pre_grad, staged, out_wide, wide
):
    lat = lax.axis_index("lat")
    windows = [
        window(grid, dr * PITCH + dc, OUTER, 0, 2).astype(BF16) for dr, dc in OFFSETS
    ]
    forward = jnp.concatenate(
        [
            jnp.concatenate(
                [
                    up_kernel[(2 * (1 - dr) + pr) * 4 + 2 * (1 - dc) + pc]
                    for pr in range(2)
                    for pc in range(2)
                ],
                axis=1,
            )
            for dr, dc in OFFSETS
        ],
        axis=0,
    )
    raw = jnp.dot(jnp.concatenate(windows, axis=1), forward, preferred_element_type=F32)
    plain = (raw + jnp.concatenate([bias[...]] * 4, axis=1)).astype(BF16).astype(F32)
    sigmoid = jax.nn.sigmoid(plain)
    activated = (plain * sigmoid).astype(BF16).astype(F32)
    cell = lax.broadcasted_iota(jnp.int32, (OUTER, 4 * COUT), 0)
    lane = lax.broadcasted_iota(jnp.int32, (OUTER, 4 * COUT), 1)
    outside = ((cell < PITCH) & (lane < 2 * COUT) & (lat == 0)) | (
        (cell >= ROWS * PITCH) & (lane >= 2 * COUT) & (lat == lat_count - 1)
    )
    keep_wide(act, jnp.where(outside, 0.0, activated))

    act_patches = patches(positions(act, INNER, 0), False)
    cot_own = window(grid, PITCH + 1, INNER, 2, TALL)
    cot_own = jnp.where(inner_mask(4 * COUT), cot_own, 0.0).astype(BF16)
    cot_stacked = jnp.concatenate([cot_own[:, i * COUT : (i + 1) * COUT] for i in range(4)], axis=0)
    mix_sum = lax.dot_general(
        act_patches, cot_stacked, (((0,), (0,)), ((), ())), preferred_element_type=F32
    )
    for w in range(4):
        for slot in range(4):
            tap = slot * 4 + w
            at = (slot // 2) * COUT
            part = jnp.zeros((LON_ALL, 8, COUT), F32)
            if tap < 9:
                part = mix_sum[tap * COUT : (tap + 1) * COUT].reshape(LON_ALL, 8, COUT)
            wide[w // 2, 2, w % 2, :, slot % 2, :, at : at + COUT] = part

    backward = jnp.concatenate([mix_kernel[i] for i in range(9)], axis=1)
    act_grad = lax.dot_general(
        patches(positions(grid, OUTER, 2), True),
        backward,
        (((1,), (1,)), ((), ())),
        preferred_element_type=F32,
    )
    slope = sigmoid * (1.0 + plain * (1.0 - sigmoid))
    graded = (beside(act_grad, OUTER) * slope).astype(BF16).astype(F32)
    keep_wide(pre_grad, jnp.where(outside, 0.0, graded))
    grad_windows = jnp.concatenate(
        [window(pre_grad, dr * PITCH + dc, INNER, 0, 4).astype(BF16) for dr, dc in OFFSETS], axis=1
    )
    in_own = window(grid, PITCH + 1, INNER, 0, 2)
    in_own = jnp.where(inner_mask(CIN), in_own, 0.0).astype(BF16)
    up_sum = lax.dot_general(
        in_own, grad_windows, (((0,), (0,)), ((), ())), preferred_element_type=F32
    )
    for dr, dc in OFFSETS:
        for pr in range(2):
            for pc in range(2):
                source = ((2 * dr + dc) * 4 + 2 * pr + pc) * COUT
                at = pc * COUT
                wide[dr, dc, pr, :, :, :, at : at + COUT] = up_sum[
                    :, source : source + COUT
                ].reshape(LON_ALL, 2, 8, COUT)
    for core in range(2):
        for part in range(PARTS):
            for x_hi in range(2):
                sums[core, part, x_hi] = wide[core, part, x_hi].reshape(CIN, SPAN).astype(BF16)

    flat_mix = mix_kernel[...].reshape(9 * COUT, COUT)
    staged[...] = jnp.dot(act_patches, flat_mix, preferred_element_type=F32)
    for s in range(2):
        for t in range(2):
            for r in range(ROWS):
                out_wide[pl.ds((2 * r + s) * 2 * COLS + t, COLS, stride=2), :] = staged[
                    pl.ds((2 * s + t) * INNER + r * PITCH, COLS), :
                ]
    section[...] = out_wide[...].astype(BF16)
    back_up = jnp.concatenate(
        [
            up_kernel[(2 * dr + pr) * 4 + 2 * dc + pc]
            for dr, dc in OFFSETS
            for pr in range(2)
            for pc in range(2)
        ],
        axis=1,
    )
    spread = lax.dot_general(
        grad_windows, back_up, (((1,), (1,)), ((), ())), preferred_element_type=F32
    )
    for i in range(2):
        act[i, :INNER, :] = spread[:, i * COUT : (i + 1) * COUT]
        for r in range(ROWS):
            input_grad[r * COLS : (r + 1) * COLS, i * COUT : (i + 1) * COUT] = act[
                i, pl.ds(r * PITCH, COLS), :
            ]


def reduce_partners(lat, lon, z_count, y_count):
    core, x_hi, z = lax.rem(lat, 2), lax.rem(lat // 2, 2), lat // 4
    y, x_lo = lax.rem(lon, y_count), lon // y_count
    return core, x_hi, z, y, x_lo


def fetch(src, dst, send, recv, to):
    copy = pltpu.make_async_remote_copy(
        src_ref=src, dst_ref=dst, send_sem=send, recv_sem=recv, device_id=to, device_id_type=MESH
    )
    copy.start()


def await_bytes(ref, sem):
    pltpu.make_async_copy(ref, ref, sem).wait()


def reduce_kernel(
    z_count,
    y_count,
    scale,
    sums,
    final,
    core_in,
    x_out,
    x_in,
    y_out,
    y_in,
    z_out,
    z_in,
    z_all,
    core_sem,
    x_sem,
    y_sem,
    z_sem,
):
    lat, lon = lax.axis_index("lat"), lax.axis_index("lon")
    core, x_hi, z, y, x_lo = reduce_partners(lat, lon, z_count, y_count)
    x = 2 * x_hi + x_lo
    own = 2 * core + x_hi

    def across_x(step):
        other = lax.rem(x + step, 4)
        return (4 * z + 2 * (other // 2) + core, (other % 2) * y_count + y), other

    def across_y(step):
        other = lax.rem(y + step, y_count)
        return (lat, x_lo * y_count + other), other

    def across_z(step):
        other = lax.rem(z + step, z_count)
        return (4 * other + 2 * x_hi + core, lon), other

    def across_inner(step):
        other = lax.rem(own + step, 4)
        return (4 * z + 2 * (other % 2) + other // 2, lon), other

    barrier = pltpu.get_barrier_semaphore()

    def greet(to):
        pl.semaphore_signal(barrier, inc=1, device_id=to, device_id_type=MESH)

    total = 0
    for count, reach in ((4, across_x), (y_count, across_y), (z_count, across_z), (4, across_inner)):
        for step in range(1, count):
            greet(reach(step)[0])
        total += count - 1
    pl.semaphore_wait(barrier, total)

    partner = (lat + 1 - 2 * core, lon)
    for part in range(PARTS):
        fetch(sums.at[1 - core, part], core_in.at[part], core_sem.at[0, part], core_sem.at[1, part], partner)
    for part in range(PARTS):
        await_bytes(core_in.at[part], core_sem.at[1, part])
        x_out[part] = (
            (sums[core, part].astype(F32) + core_in[part].astype(F32))
            .astype(BF16)
            .reshape(x_out.shape[1:])
        )
        for step in range(1, 4):
            to, other = across_x(step)
            fetch(
                x_out.at[part, other // 2, other % 2],
                x_in.at[part, step - 1],
                x_sem.at[0, part],
                x_sem.at[1, part],
                to,
            )
    for part in range(PARTS):
        await_bytes(x_in.at[part], x_sem.at[1, part])
        total = x_out[part, x_hi, x_lo].astype(F32)
        for step in range(3):
            total = total + x_in[part, step].astype(F32)
        y_out[part] = total.astype(BF16).reshape(y_out.shape[1:])
        for step in range(1, y_count):
            to, other = across_y(step)
            fetch(y_out.at[part, other], y_in.at[part, step - 1], y_sem.at[0, part], y_sem.at[1, part], to)
    per = TILES // z_count
    for part in range(PARTS):
        await_bytes(y_in.at[part], y_sem.at[1, part])
        total = y_out[part, y].astype(F32)
        for step in range(y_count - 1):
            total = total + y_in[part, step].astype(F32)
        for i in range(2):
            for half in range(2):
                tile = part * 4 + i * 2 + half
                z_out[tile // per, tile % per] = total[half * 8 : half * 8 + 8, i * COUT : (i + 1) * COUT]
    for step in range(1, z_count):
        to, other = across_z(step)
        fetch(z_out.at[other], z_in.at[step - 1], z_sem.at[0], z_sem.at[1], to)
    await_bytes(z_in, z_sem.at[1])
    total = z_out[z]
    for step in range(z_count - 1):
        total = total + z_in[step]
    z_all[z] = total * scale
    for step in range(1, z_count):
        to, _ = across_z(step)
        fetch(z_all.at[z], z_all.at[z], z_sem.at[2], z_sem.at[3], to)
    await_bytes(z_all.at[pl.ds(0, z_count - 1)], z_sem.at[3])
    for step in range(1, 4):
        to, _ = across_inner(step)
        fetch(z_all, final.at[own], z_sem.at[4], z_sem.at[5], to)
    final[own] = z_all[...]
    for part in range(PARTS):
        await_bytes(core_in.at[part], core_sem.at[0, part])
        await_bytes(x_in.at[part], x_sem.at[0, part])
        await_bytes(y_in.at[part], y_sem.at[0, part])
    await_bytes(z_in, z_sem.at[0])
    await_bytes(z_all.at[pl.ds(0, z_count - 1)], z_sem.at[2])
    await_bytes(final.at[pl.ds(0, 3)], z_sem.at[4])
    await_bytes(final.at[pl.ds(0, 3)], z_sem.at[5])


def vmem(count):
    return [pl.BlockSpec(memory_space=pltpu.VMEM)] * count


def shards(elem_codes, block_exps, up_kernel, up_bias, mix_kernel, cotangent):
    lat_count, lon_count = lax.axis_size("lat"), lax.axis_size("lon")
    y_count, z_count = lon_count // 2, lat_count // 4
    per = TILES // z_count
    limit = 48 * 2**20
    grid = pl.pallas_call(
        functools.partial(halo_kernel, lat_count, lon_count),
        out_shape=jax.ShapeDtypeStruct((TALL, FLAT, COUT), F32),
        in_specs=vmem(3),
        out_specs=vmem(1)[0],
        scratch_shapes=[
            pltpu.VMEM((TALL, CELLS, COUT), F32),
            pltpu.VMEM((4 * CELLS, COUT), F32),
            pltpu.VMEM((2, TALL // 2, 2 * COLS, COUT), BF16),
            pltpu.VMEM((2, TALL, ROWS, COUT), BF16),
            pltpu.VMEM((4, 8, COUT), F32),
            pltpu.VMEM((2, TALL // 2, 2 * COLS, COUT), BF16),
            pltpu.VMEM((2, TALL, ROWS, COUT), BF16),
            pltpu.VMEM((4, 8, COUT), F32),
            pltpu.SemaphoreType.DMA((8,)),
            pltpu.SemaphoreType.DMA((8,)),
        ],
        compiler_params=pltpu.CompilerParams(
            collective_id=0, has_side_effects=True, vmem_limit_bytes=limit
        ),
    )(
        elem_codes.reshape(CELLS, CIN),
        block_exps.reshape(CELLS, CIN // 32),
        cotangent.reshape(4 * CELLS, COUT),
    )
    section, input_grad, sums = pl.pallas_call(
        functools.partial(compute_kernel, lat_count),
        out_shape=(
            jax.ShapeDtypeStruct((4 * CELLS, COUT), BF16),
            jax.ShapeDtypeStruct((CELLS, CIN), F32),
            jax.ShapeDtypeStruct((2, PARTS, 2, CIN, SPAN), BF16),
        ),
        in_specs=vmem(4),
        out_specs=vmem(3),
        scratch_shapes=[
            pltpu.VMEM((4, FLAT, COUT), F32),
            pltpu.VMEM((4, FLAT, COUT), F32),
            pltpu.VMEM((4 * INNER, COUT), F32),
            pltpu.VMEM((4 * CELLS, COUT), F32),
            pltpu.VMEM((2, PARTS, 2, LON_ALL, 2, 8, SPAN), F32),
        ],
        compiler_params=pltpu.CompilerParams(vmem_limit_bytes=limit),
    )(
        grid,
        up_kernel.reshape(16, CIN, COUT),
        up_bias.reshape(1, COUT),
        mix_kernel.reshape(9, COUT, COUT),
    )
    out_cells = 4 * CELLS * lat_count * lon_count
    final = pl.pallas_call(
        functools.partial(reduce_kernel, z_count, y_count, 1.0 / math.sqrt(out_cells)),
        out_shape=jax.ShapeDtypeStruct((4, z_count, per, 8, COUT), F32),
        in_specs=vmem(1),
        out_specs=vmem(1)[0],
        scratch_shapes=[
            pltpu.VMEM((PARTS, 2, CIN, SPAN), BF16),
            pltpu.VMEM((PARTS, 2, 2, CIN // 2, SPAN), BF16),
            pltpu.VMEM((PARTS, 3, CIN // 2, SPAN), BF16),
            pltpu.VMEM((PARTS, y_count, 16, SPAN), BF16),
            pltpu.VMEM((PARTS, y_count - 1, 16, SPAN), BF16),
            pltpu.VMEM((z_count, per, 8, COUT), F32),
            pltpu.VMEM((z_count - 1, per, 8, COUT), F32),
            pltpu.VMEM((z_count, per, 8, COUT), F32),
            pltpu.SemaphoreType.DMA((2, PARTS)),
            pltpu.SemaphoreType.DMA((2, PARTS)),
            pltpu.SemaphoreType.DMA((2, PARTS)),
            pltpu.SemaphoreType.DMA((6,)),
        ],
        compiler_params=pltpu.CompilerParams(
            collective_id=1, has_side_effects=True, vmem_limit_bytes=limit
        ),
    )(sums)
    final = final.reshape(4, TILES, 8, COUT)
    up_part = final[:, :8].reshape(4, 4, CIN // lon_count, COUT)
    mix_part = jnp.stack([final[tap % 4, 8 + tap // 4] for tap in range(9)])
    return (
        section.reshape(2 * ROWS, 2 * COLS, COUT),
        input_grad.reshape(ROWS, COLS, CIN),
        up_part,
        mix_part.reshape(3, 3, 8, COUT),
    )


def solution(mesh):
    placed = (P("lat", "lon", None), P("lat", "lon", None), P(), P(), P(), P("lat", "lon", None))
    return jax.shard_map(
        shards,
        mesh=mesh,
        in_specs=placed,
        out_specs=(
            P("lat", "lon", None),
            P("lat", "lon", None),
            P(None, None, "lon", None),
            P(None, None, "lon", None),
        ),
        check_vma=False,
    )
```

time: 601 us -> 72 us (0.12)
  waiting for transfers between devices: 497 us -> 0 us
  Pallas kernels: 0 us -> 64.7 us
  starting transfers between devices: 59.2 us -> 0 us
  between operations: 14.8 us -> 0.75 us
  local copies, waits for them, and re-layouts: 19.8 us -> 6.18 us
  matrix products: 7.65 us -> 0 us
    psum x1 -> x0, waiting for transfers between devices: 493 us -> none  [shards(): summed = lax.psum((up_grad, mix_grad), ('lat', 'lon'))]
    pallas_call x0 -> x3, Pallas kernels: none -> 64.7 us  [the longest x1 38.6 us: shards(): pl.pallas_call(functools.partial(reduce_kernel, z_count, y_count, 1.0 / m...]
    ppermute x16 -> x0, starting transfers between devices: 59.2 us -> none  [the longest x8 31.2 us: padded_2(): after = lax.ppermute(leading, axis, down)]
    dot_general x9 -> x0, matrix products: 7.65 us -> none  [the longest x1 2.1 us: shards(): jnp.einsum('rck,kn->rcn', patches, mix_flat, preferred_element_type=jnp.f...]
    slice x22 -> x1, local copies, waits for them, and re-layouts: 7.11 us -> 0.66 us  [shards(): up_part = final[:, :8].reshape(4, 4, CIN // lon_count, COUT)]
  transfers between devices with their start and end apart: 17 -> 0, of which waited for: 2 -> 0; matrix products, arithmetic and copies ran while one was open for 2% -> 0% of each run, Pallas kernels for 0% -> 0%
where the time goes in v1:
time: 72 us; the launch traced here: 71.7 us
  Pallas kernels  64.7 us (90%)
  local copies, waits for them, and re-layouts  6.18 us (9%)
  between operations  0.75 us (1%)
    pallas_call x1, Pallas kernels, shards(): pl.pallas_call(functools.partial(reduce_kernel, z_count, y_count, 1.0 / m...  38.6 us
    pallas_call x1, Pallas kernels, shards(): pl.pallas_call(functools.partial(halo_kernel, lat_count, lon_count), out_...  22.7 us
    unnamed x21, local copies, waits for them, and re-layouts  5.51 us
    pallas_call x1, Pallas kernels, shards(): pl.pallas_call(functools.partial(compute_kernel, lat_count), out_shape=(j...  3.35 us

profile of v1, /device:TPU:1, one launch (start us, length us, event | category | flops | bytes accessed | tf_op | source)
XLA Modules:
  0.0 71.7 jit_solution(11141234693432553229)
XLA Ops:
  0.6 0.8 %copy.10 = s32[16,8,8]{2,1,0:T(8,128)S(1)} copy(s32[16,8,8]{0,2,1:T(8,128)} %param.7) | data formatting | bytes 8192 | tf_op args[1]
  1.5 0.0 copy-start.2
  1.5 0.9 %copy-done.2 = s32[16,8,256]{2,1,0:T(8,128)S(1)} copy-done((s32[16,8,256]{2,1,0:T(8,128)S(1)}, s32[16,8,256]{2,1,0:T(8,128)}, u32[]{:S(2)}) %copy-start.2) | copy-done | bytes 131096
  2.4 0.0 copy-start.3
  2.4 0.9 %copy-done.3 = bf16[32,16,128]{2,1,0:T(8,128)(2,1)S(1)} copy-done((bf16[32,16,128]{2,1,0:T(8,128)(2,1)S(1)}, bf16[32,16,128]{2,1,0:T(8,128)(2,1)}, u32[]{:S(2)}) %copy-start.3) | copy-done | bytes 131096
  3.3 22.7 %shard_map.93.grid = f32[6,192,128]{2,1,0:T(8,128)S(1)} custom-call(s32[128,256]{1,0:T(8,128)S(1)} %bitcast.60, s32[128,8]{1,0:T(8,128)S(1)} %bitcast.59, bf16[512,128]{1,0:T(8,128)(2,1)S(1)} %bitcast.61), custom_call_target="tpu_custom_call" | custom-call | tf_op jit(solution)/shard_map/pallas_call | solution.py:467
  26.0 0.0 copy-start
  26.0 1.2 %copy-done = bf16[4,4,256,128]{3,2,1,0:T(8,128)(2,1)S(1)} copy-done((bf16[4,4,256,128]{3,2,1,0:T(8,128)(2,1)S(1)}, bf16[4,4,256,128]{3,2,1,0:T(8,128)(2,1)}, u32[]{:S(2)}) %copy-start) | copy-done | bytes 1048600
  27.3 0.0 copy-start.1
  27.3 1.0 %copy-done.1 = bf16[3,3,128,128]{3,2,1,0:T(8,128)(2,1)S(1)} copy-done((bf16[3,3,128,128]{3,2,1,0:T(8,128)(2,1)S(1)}, bf16[3,3,128,128]{3,2,1,0:T(8,128)(2,1)}, u32[]{:S(2)}) %copy-start.1) | copy-done | bytes 294936
  28.2 0.0 copy-start.4
  28.2 0.7 copy-done.4
  28.9 3.4 %shard_map.94 = (bf16[512,128]{1,0:T(8,128)(2,1)}, f32[128,256]{1,0:T(8,128)}, bf16[2,3,2,256,256]{4,3,2,1,0:T(8,128)(2,1)S(1)}) custom-call(f32[6,192,128]{2,1,0:T(8,128)S(1)} %shard_map.93.grid, bf16[16,256,128]{2,1,0:T(8,128)(2,1)S(1)} %bitcast.47, f32[1,128]{1,0:T(1,128)S(1)} %bitcast.62, bf16[9,128,128]{2,1,0:T(8,128)(2,1)S(1)} %bitcast.58), custom_call_target="tpu_custom_call" | custom-call | tf_op jit(solution)/shard_map/pallas_call | solution.py:492
  32.2 38.6 %shard_map.95 = f32[4,12,1,8,128]{4,3,2,1,0:T(8,128)S(1)} custom-call(bf16[2,3,2,256,256]{4,3,2,1,0:T(8,128)(2,1)S(1)} %get-tuple-element.9.sums), custom_call_target="tpu_custom_call" | custom-call | tf_op jit(solution)/shard_map/pallas_call | solution.py:516
  71.0 0.0 copy-start.5
  71.0 0.7 slice.40
  71.7 0.0 copy-done.5
  (9 shorter events, 0.0 us)
Async XLA Ops:
  1.5 0.9 %copy-start.2 = (s32[16,8,256]{2,1,0:T(8,128)S(1)}, s32[16,8,256]{2,1,0:T(8,128)}, u32[]{:S(2)}) copy-start(s32[16,8,256]{2,1,0:T(8,128)} %param.6) | copy-start | bytes 393220
  2.4 0.9 %copy-start.3 = (bf16[32,16,128]{2,1,0:T(8,128)(2,1)S(1)}, bf16[32,16,128]{2,1,0:T(8,128)(2,1)}, u32[]{:S(2)}) copy-start(bf16[32,16,128]{2,1,0:T(8,128)(2,1)} %param.11) | copy-start | bytes 393220
  26.0 1.2 %copy-start = (bf16[4,4,256,128]{3,2,1,0:T(8,128)(2,1)S(1)}, bf16[4,4,256,128]{3,2,1,0:T(8,128)(2,1)}, u32[]{:S(2)}) copy-start(bf16[4,4,256,128]{3,2,1,0:T(8,128)(2,1)} %param.8) | copy-start | bytes 3145732
  27.3 1.0 %copy-start.1 = (bf16[3,3,128,128]{3,2,1,0:T(8,128)(2,1)S(1)}, bf16[3,3,128,128]{3,2,1,0:T(8,128)(2,1)}, u32[]{:S(2)}) copy-start(bf16[3,3,128,128]{3,2,1,0:T(8,128)(2,1)} %param.10) | copy-start | bytes 884740
  28.2 0.7 copy-start.4
  71.0 0.7 copy-start.5

commit v2 on v1

v2 whole, which is shorter than its diff:
```python
import functools
import math

import jax
import jax.numpy as jnp
from jax import lax
from jax.experimental import pallas as pl
from jax.experimental.pallas import tpu as pltpu
from jax.sharding import PartitionSpec as P

CIN = 256
COUT = 128
BLOCK = 32
ROWS = 16
COLS = 8
PITCH = 10
CELLS = ROWS * COLS
TALL = CIN // COUT + 4
FLAT = 192
OUTER = 176
INNER = ROWS * PITCH
PARTS = 3
SPAN = 2 * COUT
MIX = 2
ORDER = (2, 0, 1)
LON_ALL = 16
MESH = pl.DeviceIdType.MESH
F32 = jnp.float32
BF16 = jnp.bfloat16


def power_bits(value, bits):
    total = jnp.where(value & 1 != 0, 2.0, 1.0)
    for bit in range(1, bits):
        total = total * jnp.where(value & (1 << bit) != 0, float(1 << (1 << bit)), 1.0)
    return total


def decode(codes, factor):
    sign = jnp.where(codes >= 128, -(2.0**-9), 2.0**-9)
    fraction = (8 + (codes & 7)).astype(F32) * 0.125
    return sign * power_bits((codes >> 3) & 15, 4) * fraction * factor


def block_factors(exps, own):
    factor = power_bits(exps + 2, 2).astype(BF16)
    count = exps.shape[0]
    lane = lax.broadcasted_iota(jnp.int32, (count, COLS * CIN), 1)
    row = lax.broadcasted_iota(jnp.int32, (count, COLS * CIN), 0)
    spread = jnp.where(lane // BLOCK == row, 1.0, 0.0).astype(BF16)
    wide = lax.dot_general(factor, spread, (((0,), (0,)), ((), ())), preferred_element_type=F32)
    for c in range(COLS):
        for i in range(CIN // COUT):
            at = c * CIN + i * COUT
            own[i, pl.ds(c, ROWS, stride=COLS), :] = wide[:, at : at + COUT]


def halo_partners(lat, lon, lat_count, lon_count):
    up, down = lax.rem(lat + lat_count - 1, lat_count), lax.rem(lat + 1, lat_count)
    left, right = lax.rem(lon + lon_count - 1, lon_count), lax.rem(lon + 1, lon_count)
    return up, down, left, right


def halo_fill(codes, exps, cot, grid, own, cot_wide, row_out, col_out, corner_out):
    block_factors(exps[...], own)
    for i in range(CIN // COUT):
        own[i] = decode(codes[:, i * COUT : (i + 1) * COUT], own[i])
    cot_wide[...] = cot[...].astype(F32)
    for r in range(ROWS):
        for s in range(2):
            for t in range(2):
                own[2 + 2 * s + t, r * COLS : (r + 1) * COLS, :] = cot_wide[
                    pl.ds((2 * r + s) * 2 * COLS + t, COLS, stride=2), :
                ]
    for side, r in enumerate((ROWS - 1, 0)):
        for i in range(TALL // 2):
            row_out[side, i] = jnp.concatenate(
                [own[j, r * COLS : (r + 1) * COLS, :] for j in (2 * i, 2 * i + 1)], axis=0
            ).astype(BF16)
    for side, c in enumerate((COLS - 1, 0)):
        for i in range(TALL):
            col_out[side, i] = own[i, pl.ds(c, ROWS, stride=COLS), :].astype(BF16)
    for corner, (r, c) in enumerate(((ROWS - 1, COLS - 1), (ROWS - 1, 0), (0, COLS - 1), (0, 0))):
        cell = r * COLS + c
        corner_out[corner] = jnp.zeros((8, COUT), F32)
        for i in range(TALL):
            corner_out[corner, i : i + 1, :] = own[i, cell : cell + 1, :]
    for r in range(ROWS):
        at = (r + 1) * PITCH + 1
        for i in range(TALL):
            grid[i, at : at + COLS, :] = own[i, r * COLS : (r + 1) * COLS, :]
    tail = (ROWS + 2) * PITCH
    for i in range(TALL):
        grid[i, tail:FLAT, :] = jnp.zeros((FLAT - tail, COUT), F32)


def halo_copies(partners, lat, lon, row_out, col_out, corner_out, row_in, col_in, corner_in, send, recv):
    up, down, left, right = partners
    plan = [
        (row_out.at[0], row_in.at[0], down, lon),
        (row_out.at[1], row_in.at[1], up, lon),
        (col_out.at[0], col_in.at[0], lat, right),
        (col_out.at[1], col_in.at[1], lat, left),
        (corner_out.at[0], corner_in.at[0], down, right),
        (corner_out.at[1], corner_in.at[1], down, left),
        (corner_out.at[2], corner_in.at[2], up, right),
        (corner_out.at[3], corner_in.at[3], up, left),
    ]
    return [
        pltpu.make_async_remote_copy(
            src_ref=src,
            dst_ref=dst,
            send_sem=send.at[i],
            recv_sem=recv.at[i],
            device_id=(to_lat, to_lon),
            device_id_type=MESH,
        )
        for i, (src, dst, to_lat, to_lon) in enumerate(plan)
    ]


def halo_place(lat, lat_count, grid, row_in, col_in, corner_in):
    above = (lat > 0).astype(F32)
    below = (lat < lat_count - 1).astype(F32)
    for side, (r, keep) in enumerate(((0, above), (ROWS + 1, below))):
        at = r * PITCH + 1
        for i in range(TALL // 2):
            part = row_in[side, i].astype(F32) * keep
            grid[2 * i, at : at + COLS, :] = part[:COLS]
            grid[2 * i + 1, at : at + COLS, :] = part[COLS:]
    for side, c in enumerate((0, COLS + 1)):
        for i in range(TALL):
            grid[i, pl.ds(PITCH + c, ROWS, stride=PITCH), :] = col_in[side, i].astype(F32)
    places = ((0, 0, above), (0, COLS + 1, above), (ROWS + 1, 0, below), (ROWS + 1, COLS + 1, below))
    for corner, (r, c, keep) in enumerate(places):
        cell = r * PITCH + c
        for i in range(TALL):
            grid[i, cell : cell + 1, :] = corner_in[corner, i : i + 1, :] * keep


OFFSETS = ((0, 0), (0, 1), (1, 0), (1, 1))


def positions(ref, length, low):
    found = {}
    for dr, dc in OFFSETS:
        for pr in range(2):
            for pc in range(2):
                found[2 * dr + pr, 2 * dc + pc] = ref[
                    low + 2 * pr + pc, pl.ds(dr * PITCH + dc, length), :
                ].astype(BF16)
    return found


def window(ref, start, length, low, high):
    return jnp.concatenate([ref[i, pl.ds(start, length), :] for i in range(low, high)], axis=1)


def keep_wide(ref, value):
    for i in range(4):
        ref[i, :OUTER, :] = value[:, i * COUT : (i + 1) * COUT]
        ref[i, OUTER:, :] = jnp.zeros((FLAT - OUTER, COUT), F32)


def patches(found, flipped):
    stacked = []
    for s in range(2):
        for t in range(2):
            pieces = []
            for ky in range(3):
                for kx in range(3):
                    at = (s - ky + 2, t - kx + 2) if flipped else (s + ky, t + kx)
                    pieces.append(found[at])
            stacked.append(jnp.concatenate(pieces, axis=1))
    return jnp.concatenate(stacked, axis=0)


def beside(array, rows):
    return jnp.concatenate([array[i * rows : (i + 1) * rows] for i in range(4)], axis=1)


def inner_mask(lanes):
    cell = lax.broadcasted_iota(jnp.int32, (INNER, lanes), 0)
    return lax.rem(cell, PITCH) < COLS


def merge_slots(even, odd):
    return jnp.concatenate([even, odd], axis=1).reshape(CIN, COUT).astype(BF16)


def forward_part(lat, lat_count, grid, up_kernel, bias, act):
    windows = [window(grid, dr * PITCH + dc, OUTER, 0, 2).astype(BF16) for dr, dc in OFFSETS]
    forward = jnp.concatenate(
        [
            jnp.concatenate(
                [
                    up_kernel[(2 * (1 - dr) + pr) * 4 + 2 * (1 - dc) + pc]
                    for pr in range(2)
                    for pc in range(2)
                ],
                axis=1,
            )
            for dr, dc in OFFSETS
        ],
        axis=0,
    )
    raw = jnp.dot(jnp.concatenate(windows, axis=1), forward, preferred_element_type=F32)
    plain = (raw + jnp.concatenate([bias[...]] * 4, axis=1)).astype(BF16).astype(F32)
    sigmoid = jax.nn.sigmoid(plain)
    activated = (plain * sigmoid).astype(BF16).astype(F32)
    cell = lax.broadcasted_iota(jnp.int32, (OUTER, 4 * COUT), 0)
    lane = lax.broadcasted_iota(jnp.int32, (OUTER, 4 * COUT), 1)
    outside = ((cell < PITCH) & (lane < 2 * COUT) & (lat == 0)) | (
        (cell >= ROWS * PITCH) & (lane >= 2 * COUT) & (lat == lat_count - 1)
    )
    keep_wide(act, jnp.where(outside, 0.0, activated))
    return sigmoid * (1.0 + plain * (1.0 - sigmoid)), outside


def mix_part_sums(grid, act_patches, sums):
    cot_own = window(grid, PITCH + 1, INNER, 2, TALL)
    cot_own = jnp.where(inner_mask(4 * COUT), cot_own, 0.0).astype(BF16)
    cot_stacked = jnp.concatenate([cot_own[:, i * COUT : (i + 1) * COUT] for i in range(4)], axis=0)
    mix_sum = lax.dot_general(
        act_patches, cot_stacked, (((0,), (0,)), ((), ())), preferred_element_type=F32
    )
    empty = jnp.zeros((LON_ALL, 8, COUT), F32)
    for w in range(4):
        slots = [empty] * 4
        for slot in range(4):
            tap = slot * 4 + w
            if tap < 9:
                slots[slot] = mix_sum[tap * COUT : (tap + 1) * COUT].reshape(LON_ALL, 8, COUT)
        for i in range(2):
            sums[w // 2, MIX, w % 2, :, i * COUT : (i + 1) * COUT] = merge_slots(
                slots[2 * i], slots[2 * i + 1]
            )


def backward_part(grid, mix_kernel, slope, outside, pre_grad):
    backward = jnp.concatenate([mix_kernel[i] for i in range(9)], axis=1)
    act_grad = lax.dot_general(
        patches(positions(grid, OUTER, 2), True),
        backward,
        (((1,), (1,)), ((), ())),
        preferred_element_type=F32,
    )
    graded = (beside(act_grad, OUTER) * slope).astype(BF16).astype(F32)
    keep_wide(pre_grad, jnp.where(outside, 0.0, graded))


def grad_window(pre_grad, dr, dc):
    return window(pre_grad, dr * PITCH + dc, INNER, 0, 4).astype(BF16)


def up_part_sums(grid, pre_grad, dc, sums):
    in_own = window(grid, PITCH + 1, INNER, 0, 2)
    in_own = jnp.where(inner_mask(CIN), in_own, 0.0).astype(BF16)
    for dr in range(2):
        up_sum = lax.dot_general(
            in_own,
            grad_window(pre_grad, dr, dc),
            (((0,), (0,)), ((), ())),
            preferred_element_type=F32,
        ).astype(BF16)
        for pr in range(2):
            sums[dr, dc, pr] = up_sum[:, pr * SPAN : (pr + 1) * SPAN]


def section_part(act_patches, mix_kernel, staged, out_wide, section):
    flat_mix = mix_kernel[...].reshape(9 * COUT, COUT)
    staged[...] = jnp.dot(act_patches, flat_mix, preferred_element_type=F32)
    for s in range(2):
        for t in range(2):
            for r in range(ROWS):
                out_wide[pl.ds((2 * r + s) * 2 * COLS + t, COLS, stride=2), :] = staged[
                    pl.ds((2 * s + t) * INNER + r * PITCH, COLS), :
                ]
    section[...] = out_wide[...].astype(BF16)


def input_part(pre_grad, up_kernel, act, input_grad):
    back_up = jnp.concatenate(
        [
            up_kernel[(2 * dr + pr) * 4 + 2 * dc + pc]
            for dr, dc in OFFSETS
            for pr in range(2)
            for pc in range(2)
        ],
        axis=1,
    )
    grad_windows = jnp.concatenate([grad_window(pre_grad, dr, dc) for dr, dc in OFFSETS], axis=1)
    spread = lax.dot_general(
        grad_windows, back_up, (((1,), (1,)), ((), ())), preferred_element_type=F32
    )
    for i in range(2):
        act[i, :INNER, :] = spread[:, i * COUT : (i + 1) * COUT]
        for r in range(ROWS):
            input_grad[r * COLS : (r + 1) * COLS, i * COUT : (i + 1) * COUT] = act[
                i, pl.ds(r * PITCH, COLS), :
            ]


def reduce_partners(lat, lon, z_count, y_count):
    core, x_hi, z = lax.rem(lat, 2), lax.rem(lat // 2, 2), lat // 4
    y, x_lo = lax.rem(lon, y_count), lon // y_count
    return core, x_hi, z, y, x_lo


def fetch(src, dst, send, recv, to):
    copy = pltpu.make_async_remote_copy(
        src_ref=src, dst_ref=dst, send_sem=send, recv_sem=recv, device_id=to, device_id_type=MESH
    )
    copy.start()


def await_bytes(ref, sem):
    pltpu.make_async_copy(ref, ref, sem).wait()


def z_plan(z_count):
    return 3, z_count // 3


def section_kernel(
    lat_count,
    lon_count,
    scale,
    codes_hbm,
    exps_hbm,
    cot_hbm,
    up_hbm,
    bias_hbm,
    mix_hbm,
    section,
    input_grad,
    up_out,
    mix_out,
    codes,
    exps,
    cot,
    up_kernel,
    bias,
    mix_kernel,
    load_sem,
    grid,
    own,
    cot_wide,
    row_out,
    col_out,
    corner_out,
    row_in,
    col_in,
    corner_in,
    halo_send,
    halo_recv,
    act,
    pre_grad,
    staged,
    out_wide,
    sums,
    core_in,
    x_out,
    xa_in,
    xb_in,
    y_out,
    y_in,
    far,
    near,
    final,
    core_sem,
    x_sem,
    y_sem,
    far_sem,
    near_sem,
    final_sem,
):
    z_count, y_count = lat_count // 4, lon_count // 2
    far_count, near_count = z_plan(z_count)
    lat, lon = lax.axis_index("lat"), lax.axis_index("lon")
    core, x_hi, z, y, x_lo = reduce_partners(lat, lon, z_count, y_count)
    x = 2 * x_hi + x_lo
    own_w = 2 * core + x_hi

    def at_x(step):
        other = lax.rem(x + step + 4, 4)
        return 4 * z + 2 * (other // 2) + core, lax.rem(other, 2) * y_count + y

    def at_y(step):
        return lat, x_lo * y_count + lax.rem(y + step, y_count)

    def at_z(step):
        return 4 * lax.rem(z + step + z_count, z_count) + 2 * x_hi + core, lon

    def at_inner(step):
        other = lax.rem(own_w + step, 4)
        return 4 * z + 2 * lax.rem(other, 2) + other // 2, lon

    partner = (lat + 1 - 2 * core, lon)
    far_steps = [near_count * i for i in range(1, far_count)]
    near_steps = [i if 2 * i <= near_count else i - near_count for i in range(1, near_count)]

    loads = [
        pltpu.make_async_copy(src, dst, load_sem.at[i])
        for i, (src, dst) in enumerate(
            (
                (exps_hbm, exps),
                (codes_hbm, codes),
                (cot_hbm, cot),
                (up_hbm, up_kernel),
                (mix_hbm, mix_kernel),
                (bias_hbm, bias),
            )
        )
    ]
    for load in loads:
        load.start()

    barrier = pltpu.get_barrier_semaphore()
    up, down, left, right = partners = halo_partners(lat, lon, lat_count, lon_count)
    greeted = [(a, b) for a in (up, down) for b in (left, lon, right)] + [(lat, left), (lat, right)]
    greeted += [partner, at_x(1), at_x(-1)]
    greeted += [at_y(step) for step in range(1, y_count)]
    for step in far_steps + near_steps:
        greeted += [at_z(step), at_z(-step)]
    greeted += [at_inner(step) for step in range(1, 4)]
    for to in greeted:
        pl.semaphore_signal(barrier, inc=1, device_id=to, device_id_type=MESH)
    for load in loads[:3]:
        load.wait()
    halo_fill(codes, exps, cot, grid, own, cot_wide, row_out, col_out, corner_out)
    pl.semaphore_wait(barrier, len(greeted))
    halo = halo_copies(
        partners, lat, lon, row_out, col_out, corner_out, row_in, col_in, corner_in, halo_send, halo_recv
    )
    for copy in halo:
        copy.start()
    for load in loads[3:]:
        load.wait()
    for copy in halo:
        copy.wait_recv()
    halo_place(lat, lat_count, grid, row_in, col_in, corner_in)

    def core_start(part):
        fetch(sums.at[1 - core, part], core_in.at[part], core_sem.at[0, part], core_sem.at[1, part], partner)

    half = CIN // 4

    def x_first(part):
        await_bytes(core_in.at[part], core_sem.at[1, part])
        merged = sums[core, part].astype(F32) + core_in[part].astype(F32)
        x_out[part] = merged.astype(BF16).reshape(x_out.shape[1:])
        across = lax.rem(x + 2, 4)
        for side, step in ((0, 1), (1, -1)):
            fetch(
                x_out.at[part, across, pl.ds(side * half, half)],
                xa_in.at[part, side],
                x_sem.at[0, part, side],
                x_sem.at[1, part, side],
                at_x(step),
            )

    def x_second(part):
        for side, step in ((0, 1), (1, -1)):
            await_bytes(xa_in.at[part, side], x_sem.at[1, part, side])
            beside_x = lax.rem(x + step + 4, 4)
            rows = pl.ds(side * half, half)
            merged = x_out[part, beside_x, rows].astype(F32) + xa_in[part, side].astype(F32)
            x_out[part, beside_x, rows] = merged.astype(BF16)
            fetch(
                x_out.at[part, beside_x],
                xb_in.at[part, side],
                x_sem.at[2, part, side],
                x_sem.at[3, part, side],
                at_x(step),
            )

    def y_start(part):
        for side in range(2):
            await_bytes(xb_in.at[part, side], x_sem.at[3, part, side])
        merged = x_out[part, x].astype(F32) + xb_in[part, 0].astype(F32) + xb_in[part, 1].astype(F32)
        y_out[part] = merged.astype(BF16).reshape(y_out.shape[1:])
        for step in range(1, y_count):
            fetch(
                y_out.at[part, lax.rem(y + step, y_count)],
                y_in.at[part, step - 1],
                y_sem.at[0, part],
                y_sem.at[1, part],
                at_y(step),
            )

    far_at, near_at = z // near_count, lax.rem(z, near_count)

    def far_start(part):
        await_bytes(y_in.at[part], y_sem.at[1, part])
        total = y_out[part, y].astype(F32)
        for step in range(y_count - 1):
            total = total + y_in[part, step].astype(F32)
        far[part, far_at] = total.astype(BF16)
        for step in far_steps:
            fetch(far.at[part, far_at], far.at[part, far_at], far_sem.at[0, part], far_sem.at[1, part], at_z(step))

    def near_start(part):
        await_bytes(far.at[part, pl.ds(0, far_count - 1)], far_sem.at[1, part])
        total = far[part, 0].astype(F32)
        for i in range(1, far_count):
            total = total + far[part, i].astype(F32)
        near[part, near_at] = total.astype(BF16)
        for step in near_steps:
            fetch(
                near.at[part, near_at], near.at[part, near_at], near_sem.at[0, part], near_sem.at[1, part], at_z(step)
            )

    def final_start(part):
        if near_count > 1:
            await_bytes(near.at[part, pl.ds(0, near_count - 1)], near_sem.at[1, part])
        total = near[part, 0].astype(F32)
        for i in range(1, near_count):
            total = total + near[part, i].astype(F32)
        final[part, own_w] = (total * scale).astype(BF16)
        for step in range(1, 4):
            fetch(
                final.at[part, own_w],
                final.at[part, own_w],
                final_sem.at[0, part],
                final_sem.at[1, part],
                at_inner(step),
            )

    def finish(part):
        await_bytes(final.at[part, pl.ds(0, 3)], final_sem.at[1, part])
        for w in range(4):
            total = final[part, w].astype(F32)
            for i in range(2):
                piece = total[:, i * COUT : (i + 1) * COUT]
                if part != MIX:
                    up_out[w, 2 * part + i] = piece
                    continue
                for slot in range(2):
                    tap = (2 * i + slot) * 4 + w
                    if tap < 9:
                        mix_out[tap] = piece[slot * 8 : slot * 8 + 8]

    slope, outside = forward_part(lat, lat_count, grid, up_kernel, bias, act)
    act_patches = patches(positions(act, INNER, 0), False)
    mix_part_sums(grid, act_patches, sums)
    core_start(MIX)
    backward_part(grid, mix_kernel, slope, outside, pre_grad)
    for dc in range(2):
        up_part_sums(grid, pre_grad, dc, sums)
        core_start(dc)
    for part in ORDER:
        x_first(part)
    x_second(ORDER[0])
    section_part(act_patches, mix_kernel, staged, out_wide, section)
    x_second(ORDER[1])
    x_second(ORDER[2])
    y_start(ORDER[0])
    input_part(pre_grad, up_kernel, act, input_grad)
    y_start(ORDER[1])
    far_start(ORDER[0])
    y_start(ORDER[2])
    far_start(ORDER[1])
    near_start(ORDER[0])
    far_start(ORDER[2])
    near_start(ORDER[1])
    final_start(ORDER[0])
    near_start(ORDER[2])
    final_start(ORDER[1])
    finish(ORDER[0])
    final_start(ORDER[2])
    finish(ORDER[1])
    for copy in halo:
        copy.wait_send()
    for part in range(PARTS):
        await_bytes(core_in.at[part], core_sem.at[0, part])
        for side in range(2):
            await_bytes(xa_in.at[part, side], x_sem.at[0, part, side])
            await_bytes(xb_in.at[part, side], x_sem.at[2, part, side])
        await_bytes(y_in.at[part], y_sem.at[0, part])
        await_bytes(far.at[part, pl.ds(0, far_count - 1)], far_sem.at[0, part])
        if near_count > 1:
            await_bytes(near.at[part, pl.ds(0, near_count - 1)], near_sem.at[0, part])
        await_bytes(final.at[part, pl.ds(0, 3)], final_sem.at[0, part])
    finish(ORDER[2])


def shards(elem_codes, block_exps, up_kernel, up_bias, mix_kernel, cotangent):
    lat_count, lon_count = lax.axis_size("lat"), lax.axis_size("lon")
    y_count, z_count = lon_count // 2, lat_count // 4
    far_count, near_count = z_plan(z_count)
    out_cells = 4 * CELLS * lat_count * lon_count
    operands = (
        elem_codes.reshape(CELLS, CIN),
        block_exps.transpose(1, 2, 0).reshape(COLS * CIN // BLOCK, ROWS),
        cotangent.reshape(4 * CELLS, COUT),
        up_kernel.reshape(16, CIN, COUT),
        up_bias.reshape(1, COUT),
        mix_kernel.reshape(9, COUT, COUT),
    )
    dma = pltpu.SemaphoreType.DMA
    section, input_grad, up_part, mix_part = pl.pallas_call(
        functools.partial(section_kernel, lat_count, lon_count, 1.0 / math.sqrt(out_cells)),
        out_shape=(
            jax.ShapeDtypeStruct((4 * CELLS, COUT), BF16),
            jax.ShapeDtypeStruct((CELLS, CIN), F32),
            jax.ShapeDtypeStruct((4, 4, LON_ALL, COUT), F32),
            jax.ShapeDtypeStruct((9, 8, COUT), F32),
        ),
        in_specs=[pl.BlockSpec(memory_space=pltpu.HBM)] * 6,
        out_specs=[pl.BlockSpec(memory_space=pltpu.VMEM)] * 4,
        scratch_shapes=[pltpu.VMEM(operand.shape, operand.dtype) for operand in operands]
        + [
            dma((6,)),
            pltpu.VMEM((TALL, FLAT, COUT), F32),
            pltpu.VMEM((TALL, CELLS, COUT), F32),
            pltpu.VMEM((4 * CELLS, COUT), F32),
            pltpu.VMEM((2, TALL // 2, 2 * COLS, COUT), BF16),
            pltpu.VMEM((2, TALL, ROWS, COUT), BF16),
            pltpu.VMEM((4, 8, COUT), F32),
            pltpu.VMEM((2, TALL // 2, 2 * COLS, COUT), BF16),
            pltpu.VMEM((2, TALL, ROWS, COUT), BF16),
            pltpu.VMEM((4, 8, COUT), F32),
            dma((8,)),
            dma((8,)),
            pltpu.VMEM((4, FLAT, COUT), F32),
            pltpu.VMEM((4, FLAT, COUT), F32),
            pltpu.VMEM((4 * INNER, COUT), F32),
            pltpu.VMEM((4 * CELLS, COUT), F32),
            pltpu.VMEM((2, PARTS, 2, CIN, SPAN), BF16),
            pltpu.VMEM((PARTS, 2, CIN, SPAN), BF16),
            pltpu.VMEM((PARTS, 4, CIN // 2, SPAN), BF16),
            pltpu.VMEM((PARTS, 2, CIN // 4, SPAN), BF16),
            pltpu.VMEM((PARTS, 2, CIN // 2, SPAN), BF16),
            pltpu.VMEM((PARTS, y_count, 16, SPAN), BF16),
            pltpu.VMEM((PARTS, y_count - 1, 16, SPAN), BF16),
            pltpu.VMEM((PARTS, far_count, 16, SPAN), BF16),
            pltpu.VMEM((PARTS, near_count, 16, SPAN), BF16),
            pltpu.VMEM((PARTS, 4, 16, SPAN), BF16),
            dma((2, PARTS)),
            dma((4, PARTS, 2)),
            dma((2, PARTS)),
            dma((2, PARTS)),
            dma((2, PARTS)),
            dma((2, PARTS)),
        ],
        compiler_params=pltpu.CompilerParams(
            collective_id=0, has_side_effects=True, vmem_limit_bytes=56 * 2**20
        ),
    )(*operands)
    return (
        section.reshape(2 * ROWS, 2 * COLS, COUT),
        input_grad.reshape(ROWS, COLS, CIN),
        up_part,
        mix_part.reshape(3, 3, 8, COUT),
    )


def solution(mesh):
    placed = (P("lat", "lon", None), P("lat", "lon", None), P(), P(), P(), P("lat", "lon", None))
    return jax.shard_map(
        shards,
        mesh=mesh,
        in_specs=placed,
        out_specs=(
            P("lat", "lon", None),
            P("lat", "lon", None),
            P(None, None, "lon", None),
            P(None, None, "lon", None),
        ),
        check_vma=False,
    )
```

time: 72 us -> 62.9 us (0.87)
  Pallas kernels: 64.7 us -> 58 us
  local copies, waits for them, and re-layouts: 6.18 us -> 3.94 us
    pallas_call x3 -> x1, Pallas kernels: 64.7 us -> 58 us  [shards(): pl.pallas_call(functools.partial(section_kernel, lat_count, lon_count, 1....]
    unnamed x21 -> x10, local copies, waits for them, and re-layouts: 5.51 us -> 3.94 us
where the time goes in v2:
time: 62.9 us; the launch traced here: 62.6 us
  Pallas kernels  58 us (92%)
  local copies, waits for them, and re-layouts  3.94 us (6%)
  between operations  0.65 us (1%)
    pallas_call x1, Pallas kernels, shards(): pl.pallas_call(functools.partial(section_kernel, lat_count, lon_count, 1....  58 us
    unnamed x10, local copies, waits for them, and re-layouts  3.94 us

profile of v2, /device:TPU:1, one launch (start us, length us, event | category | flops | bytes accessed | tf_op | source)
XLA Modules:
  0.0 62.6 jit_solution(12169218284101381978)
XLA Ops:
  0.6 58.0 %shard_map.93 = (bf16[512,128]{1,0:T(8,128)(2,1)}, f32[128,256]{1,0:T(8,128)}, f32[4,4,16,128]{3,2,1,0:T(8,128)}, f32[9,8,128]{2,1,0:T(8,128)}) custom-call(s32[128,256]{1,0:T(8,128)} %bitcast.13, s32[64,16]{1,0:T(8,128)} %bitcast.18, bf16[512,128]{1,0:T(8,128)(2,1)} %bitcast.14, bf16[16,256,128]{2,1,0:T(8,128)(2,1)} %bitcast.11, f32[1,128]{1,0:T(1,128)} %bitcast.19, ...), custom_call_target="tpu_custom_call" | custom-call | tf_op jit(solution)/shard_map/pallas_call | solution.py:602
  58.7 0.0 copy-start.1
  58.7 1.6 %copy.14 = bf16[32,16,128]{2,1,0:T(8,128)(2,1)} copy(bf16[32,16,128]{2,1,0:T(8,128)(2,1)} %bitcast.16) | data formatting | bytes 262144
  60.3 0.0 copy-done.1
  60.3 0.0 copy-start
  60.3 0.7 %copy.15 = f32[16,8,256]{2,1,0:T(8,128)} copy(f32[16,8,256]{2,1,0:T(8,128)S(1)} %bitcast.15) | data formatting | bytes 262144
  60.9 0.3 copy-done
  61.2 0.0 copy-start.2
  61.2 0.7 %copy.16 = f32[4,4,16,128]{3,2,1,0:T(8,128)} copy(f32[4,4,16,128]{3,2,1,0:T(8,128)S(1)} %copy-done) | data formatting | bytes 262144
  61.9 0.1 copy-done.2
  62.0 0.6 copy.17
Async XLA Ops:
  58.7 1.6 %copy-start.1 = (f32[128,256]{1,0:T(8,128)S(1)}, f32[128,256]{1,0:T(8,128)}, u32[]{:S(2)}) copy-start(f32[128,256]{1,0:T(8,128)} %get-tuple-element.9) | copy-start | bytes 393220
  60.3 1.0 %copy-start = (f32[4,4,16,128]{3,2,1,0:T(8,128)S(1)}, f32[4,4,16,128]{3,2,1,0:T(8,128)}, u32[]{:S(2)}) copy-start(f32[4,4,16,128]{3,2,1,0:T(8,128)} %get-tuple-element.18) | copy-start | bytes 393220
  61.2 0.8 %copy-start.2 = (f32[9,8,128]{2,1,0:T(8,128)S(1)}, f32[9,8,128]{2,1,0:T(8,128)}, u32[]{:S(2)}) copy-start(f32[9,8,128]{2,1,0:T(8,128)} %get-tuple-element.11) | copy-start | bytes 110596

commit v3 on v2

--- a/solution.py
+++ b/solution.py
@@ -380,7 +380,6 @@
     lat, lon = lax.axis_index("lat"), lax.axis_index("lon")
     core, x_hi, z, y, x_lo = reduce_partners(lat, lon, z_count, y_count)
     x = 2 * x_hi + x_lo
-    own_w = 2 * core + x_hi
 
     def at_x(step):
         other = lax.rem(x + step + 4, 4)
@@ -389,12 +388,8 @@
     def at_y(step):
         return lat, x_lo * y_count + lax.rem(y + step, y_count)
 
-    def at_z(step):
-        return 4 * lax.rem(z + step + z_count, z_count) + 2 * x_hi + core, lon
-
-    def at_inner(step):
-        other = lax.rem(own_w + step, 4)
-        return 4 * z + 2 * lax.rem(other, 2) + other // 2, lon
+    def at_z(step, row):
+        return 4 * lax.rem(z + step + z_count, z_count) + 2 * row + core, lon
 
     partner = (lat + 1 - 2 * core, lon)
     far_steps = [near_count * i for i in range(1, far_count)]
@@ -421,9 +416,10 @@
     greeted = [(a, b) for a in (up, down) for b in (left, lon, right)] + [(lat, left), (lat, right)]
     greeted += [partner, at_x(1), at_x(-1)]
     greeted += [at_y(step) for step in range(1, y_count)]
-    for step in far_steps + near_steps:
-        greeted += [at_z(step), at_z(-step)]
-    greeted += [at_inner(step) for step in range(1, 4)]
+    far_all = sorted({step % z_count for base in far_steps for step in (base, -base)})
+    near_all = sorted({step % z_count for base in near_steps for step in (base, -base)})
+    greeted += [at_z(step, x_hi) for step in far_all + near_all]
+    greeted += [at_z(step, 1 - x_hi) for step in [0] + near_all]
     for to in greeted:
         pl.semaphore_signal(barrier, inc=1, device_id=to, device_id_type=MESH)
     for load in loads[:3]:
@@ -498,41 +494,34 @@
             total = total + y_in[part, step].astype(F32)
         far[part, far_at] = total.astype(BF16)
         for step in far_steps:
-            fetch(far.at[part, far_at], far.at[part, far_at], far_sem.at[0, part], far_sem.at[1, part], at_z(step))
+            fetch(far.at[part, far_at], far.at[part, far_at], far_sem.at[0, part], far_sem.at[1, part], at_z(step, x_hi))
 
     def near_start(part):
         await_bytes(far.at[part, pl.ds(0, far_count - 1)], far_sem.at[1, part])
         total = far[part, 0].astype(F32)
         for i in range(1, far_count):
             total = total + far[part, i].astype(F32)
-        near[part, near_at] = total.astype(BF16)
-        for step in near_steps:
-            fetch(
-                near.at[part, near_at], near.at[part, near_at], near_sem.at[0, part], near_sem.at[1, part], at_z(step)
-            )
+        slot = 2 * near_at + x_hi
+        near[part, slot] = total.astype(BF16)
+        for to in [at_z(step, 1 - x_hi) for step in [0] + near_steps] + [at_z(step, x_hi) for step in near_steps]:
+            fetch(near.at[part, slot], near.at[part, slot], near_sem.at[0, part], near_sem.at[1, part], to)
 
     def final_start(part):
-        if near_count > 1:
-            await_bytes(near.at[part, pl.ds(0, near_count - 1)], near_sem.at[1, part])
-        total = near[part, 0].astype(F32)
-        for i in range(1, near_count):
-            total = total + near[part, i].astype(F32)
-        final[part, own_w] = (total * scale).astype(BF16)
-        for step in range(1, 4):
-            fetch(
-                final.at[part, own_w],
-                final.at[part, own_w],
-                final_sem.at[0, part],
-                final_sem.at[1, part],
-                at_inner(step),
-            )
+        await_bytes(near.at[part, pl.ds(0, 2 * near_count - 1)], near_sem.at[1, part])
+        for row in range(2):
+            total = near[part, row].astype(F32)
+            for i in range(1, near_count):
+                total = total + near[part, 2 * i + row].astype(F32)
+            final[part, core, row] = total * scale
+        fetch(
+            final.at[part, core], final.at[part, core], final_sem.at[0, part], final_sem.at[1, part], partner
+        )
 
     def finish(part):
-        await_bytes(final.at[part, pl.ds(0, 3)], final_sem.at[1, part])
+        await_bytes(final.at[part, 0], final_sem.at[1, part])
         for w in range(4):
-            total = final[part, w].astype(F32)
             for i in range(2):
-                piece = total[:, i * COUT : (i + 1) * COUT]
+                piece = final[part, w // 2, w % 2, :, i * COUT : (i + 1) * COUT]
                 if part != MIX:
                     up_out[w, 2 * part + i] = piece
                     continue
@@ -546,11 +535,13 @@
     mix_part_sums(grid, act_patches, sums)
     core_start(MIX)
     backward_part(grid, mix_kernel, slope, outside, pre_grad)
-    for dc in range(2):
-        up_part_sums(grid, pre_grad, dc, sums)
-        core_start(dc)
-    for part in ORDER:
-        x_first(part)
+    up_part_sums(grid, pre_grad, 0, sums)
+    core_start(0)
+    x_first(MIX)
+    up_part_sums(grid, pre_grad, 1, sums)
+    core_start(1)
+    x_first(0)
+    x_first(1)
     x_second(ORDER[0])
     section_part(act_patches, mix_kernel, staged, out_wide, section)
     x_second(ORDER[1])
@@ -579,10 +570,17 @@
             await_bytes(xb_in.at[part, side], x_sem.at[2, part, side])
         await_bytes(y_in.at[part], y_sem.at[0, part])
         await_bytes(far.at[part, pl.ds(0, far_count - 1)], far_sem.at[0, part])
-        if near_count > 1:
-            await_bytes(near.at[part, pl.ds(0, near_count - 1)], near_sem.at[0, part])
-        await_bytes(final.at[part, pl.ds(0, 3)], final_sem.at[0, part])
+        await_bytes(near.at[part, pl.ds(0, 2 * near_count - 1)], near_sem.at[0, part])
+        await_bytes(final.at[part, 0], final_sem.at[0, part])
     finish(ORDER[2])
+
+
+def write_kernel(*refs):
+    copies = [pltpu.make_async_copy(refs[i], refs[4 + i], refs[8].at[i]) for i in range(4)]
+    for copy in copies:
+        copy.start()
+    for copy in copies:
+        copy.wait()
 
 
 def shards(elem_codes, block_exps, up_kernel, up_bias, mix_kernel, cotangent):
@@ -599,7 +597,7 @@
         mix_kernel.reshape(9, COUT, COUT),
     )
     dma = pltpu.SemaphoreType.DMA
-    section, input_grad, up_part, mix_part = pl.pallas_call(
+    results = pl.pallas_call(
         functools.partial(section_kernel, lat_count, lon_count, 1.0 / math.sqrt(out_cells)),
         out_shape=(
             jax.ShapeDtypeStruct((4 * CELLS, COUT), BF16),
@@ -635,8 +633,8 @@
             pltpu.VMEM((PARTS, y_count, 16, SPAN), BF16),
             pltpu.VMEM((PARTS, y_count - 1, 16, SPAN), BF16),
             pltpu.VMEM((PARTS, far_count, 16, SPAN), BF16),
-            pltpu.VMEM((PARTS, near_count, 16, SPAN), BF16),
-            pltpu.VMEM((PARTS, 4, 16, SPAN), BF16),
+            pltpu.VMEM((PARTS, 2 * near_count, 16, SPAN), BF16),
+            pltpu.VMEM((PARTS, 2, 2, 16, SPAN), F32),
             dma((2, PARTS)),
             dma((4, PARTS, 2)),
             dma((2, PARTS)),
@@ -648,6 +646,14 @@
             collective_id=0, has_side_effects=True, vmem_limit_bytes=56 * 2**20
         ),
     )(*operands)
+    section, input_grad, up_part, mix_part = pl.pallas_call(
+        write_kernel,
+        out_shape=tuple(jax.ShapeDtypeStruct(result.shape, result.dtype) for result in results),
+        in_specs=[pl.BlockSpec(memory_space=pltpu.HBM)] * 4,
+        out_specs=[pl.BlockSpec(memory_space=pltpu.HBM)] * 4,
+        scratch_shapes=[dma((4,))],
+        compiler_params=pltpu.CompilerParams(vmem_limit_bytes=56 * 2**20),
+    )(*results)
     return (
         section.reshape(2 * ROWS, 2 * COLS, COUT),
         input_grad.reshape(ROWS, COLS, CIN),

time: 62.9 us -> 72.6 us (1.15)
  Pallas kernels: 58 us -> 71.8 us
  local copies, waits for them, and re-layouts: 3.94 us -> 0 us
    pallas_call x0 -> x1, Pallas kernels: none -> 14.2 us  [shards(): pl.pallas_call(write_kernel, out_shape=tuple((jax.ShapeDtypeStruct(result...]
    unnamed x10 -> x0, local copies, waits for them, and re-layouts: 3.94 us -> none
where the time goes in v3:
time: 72.6 us; the launch traced here: 72.4 us
  Pallas kernels  71.8 us (99%)
    pallas_call x1, Pallas kernels, shards(): pl.pallas_call(functools.partial(section_kernel, lat_count, lon_count, 1....  57.6 us
    pallas_call x1, Pallas kernels, shards(): pl.pallas_call(write_kernel, out_shape=tuple((jax.ShapeDtypeStruct(result...  14.2 us

profile of v3, /device:TPU:1, one launch (start us, length us, event | category | flops | bytes accessed | tf_op | source)
XLA Modules:
  0.0 72.4 jit_solution(14678500880041187795)
XLA Ops:
  0.6 57.6 %shard_map.93 = (bf16[512,128]{1,0:T(8,128)(2,1)}, f32[128,256]{1,0:T(8,128)}, f32[4,4,16,128]{3,2,1,0:T(8,128)}, f32[9,8,128]{2,1,0:T(8,128)}) custom-call(s32[128,256]{1,0:T(8,128)} %bitcast.13, s32[64,16]{1,0:T(8,128)} %bitcast.15, bf16[512,128]{1,0:T(8,128)(2,1)} %bitcast.14, bf16[16,256,128]{2,1,0:T(8,128)(2,1)} %bitcast.11, f32[1,128]{1,0:T(1,128)} %bitcast.16, ...), custom_call_target="tpu_custom_call" | custom-call | tf_op jit(solution)/shard_map/pallas_call | solution.py:600
  58.3 14.2 %shard_map.94 = (bf16[512,128]{1,0:T(8,128)(2,1)}, f32[128,256]{1,0:T(8,128)}, f32[4,4,16,128]{3,2,1,0:T(8,128)}, f32[9,8,128]{2,1,0:T(8,128)}) custom-call(bf16[512,128]{1,0:T(8,128)(2,1)} %get-tuple-element.12.refs_0_, f32[128,256]{1,0:T(8,128)} %get-tuple-element.13.refs_1_, f32[4,4,16,128]{3,2,1,0:T(8,128)} %get-tuple-element.14.refs_2_, ...), custom_call_target="tpu_custom_call" | custom-call | tf_op jit(solution)/shard_map/pallas_call | solution.py:649

commit v4 on v3

--- a/solution.py
+++ b/solution.py
@@ -542,25 +542,13 @@
     core_start(1)
     x_first(0)
     x_first(1)
-    x_second(ORDER[0])
     section_part(act_patches, mix_kernel, staged, out_wide, section)
-    x_second(ORDER[1])
-    x_second(ORDER[2])
-    y_start(ORDER[0])
+    for part in ORDER:
+        x_second(part)
     input_part(pre_grad, up_kernel, act, input_grad)
-    y_start(ORDER[1])
-    far_start(ORDER[0])
-    y_start(ORDER[2])
-    far_start(ORDER[1])
-    near_start(ORDER[0])
-    far_start(ORDER[2])
-    near_start(ORDER[1])
-    final_start(ORDER[0])
-    near_start(ORDER[2])
-    final_start(ORDER[1])
-    finish(ORDER[0])
-    final_start(ORDER[2])
-    finish(ORDER[1])
+    for stage in (y_start, far_start, near_start, final_start):
+        for part in ORDER:
+            stage(part)
     for copy in halo:
         copy.wait_send()
     for part in range(PARTS):
@@ -572,15 +560,13 @@
         await_bytes(far.at[part, pl.ds(0, far_count - 1)], far_sem.at[0, part])
         await_bytes(near.at[part, pl.ds(0, 2 * near_count - 1)], near_sem.at[0, part])
         await_bytes(final.at[part, 0], final_sem.at[0, part])
-    finish(ORDER[2])
+    for part in ORDER:
+        finish(part)
 
 
 def write_kernel(*refs):
-    copies = [pltpu.make_async_copy(refs[i], refs[4 + i], refs[8].at[i]) for i in range(4)]
-    for copy in copies:
-        copy.start()
-    for copy in copies:
-        copy.wait()
+    for i in range(4):
+        refs[4 + i][...] = refs[i][...]
 
 
 def shards(elem_codes, block_exps, up_kernel, up_bias, mix_kernel, cotangent):
@@ -649,9 +635,8 @@
     section, input_grad, up_part, mix_part = pl.pallas_call(
         write_kernel,
         out_shape=tuple(jax.ShapeDtypeStruct(result.shape, result.dtype) for result in results),
-        in_specs=[pl.BlockSpec(memory_space=pltpu.HBM)] * 4,
-        out_specs=[pl.BlockSpec(memory_space=pltpu.HBM)] * 4,
-        scratch_shapes=[dma((4,))],
+        in_specs=[pl.BlockSpec(memory_space=pltpu.VMEM)] * 4,
+        out_specs=[pl.BlockSpec(memory_space=pltpu.VMEM)] * 4,
         compiler_params=pltpu.CompilerParams(vmem_limit_bytes=56 * 2**20),
     )(*results)
     return (

time: 72.6 us -> 55.9 us (0.77)
  Pallas kernels: 71.8 us -> 55.1 us
    pallas_call x1, Pallas kernels: 14.2 us -> 1.79 us  [shards(): pl.pallas_call(write_kernel, out_shape=tuple((jax.ShapeDtypeStruct(result...]
    pallas_call x1, Pallas kernels: 57.6 us -> 53.3 us  [shards(): pl.pallas_call(functools.partial(section_kernel, lat_count, lon_count, 1....]
where the time goes in v4:
time: 55.9 us; the launch traced here: 55.7 us
  Pallas kernels  55.1 us (99%)
  between operations  0.64 us (1%)
    pallas_call x1, Pallas kernels, shards(): pl.pallas_call(functools.partial(section_kernel, lat_count, lon_count, 1....  53.3 us
    pallas_call x1, Pallas kernels, shards(): pl.pallas_call(write_kernel, out_shape=tuple((jax.ShapeDtypeStruct(result...  1.79 us

profile of v4, /device:TPU:1, one launch (start us, length us, event | category | flops | bytes accessed | tf_op | source)
XLA Modules:
  0.0 55.7 jit_solution(3628561247172611069)
XLA Ops:
  0.6 53.3 %shard_map.93 = (bf16[512,128]{1,0:T(8,128)(2,1)}, f32[128,256]{1,0:T(8,128)}, f32[4,4,16,128]{3,2,1,0:T(8,128)}, f32[9,8,128]{2,1,0:T(8,128)}) custom-call(s32[128,256]{1,0:T(8,128)} %bitcast.13, s32[64,16]{1,0:T(8,128)} %bitcast.15, bf16[512,128]{1,0:T(8,128)(2,1)} %bitcast.14, bf16[16,256,128]{2,1,0:T(8,128)(2,1)} %bitcast.11, f32[1,128]{1,0:T(1,128)} %bitcast.16, ...), custom_call_target="tpu_custom_call" | custom-call | tf_op jit(solution)/shard_map/pallas_call | solution.py:586
  53.9 1.8 %shard_map.94 = (bf16[512,128]{1,0:T(8,128)(2,1)}, f32[128,256]{1,0:T(8,128)}, f32[4,4,16,128]{3,2,1,0:T(8,128)}, f32[9,8,128]{2,1,0:T(8,128)}) custom-call(bf16[512,128]{1,0:T(8,128)(2,1)} %get-tuple-element.12.refs_0_, f32[128,256]{1,0:T(8,128)} %get-tuple-element.13.refs_1_, f32[4,4,16,128]{3,2,1,0:T(8,128)} %get-tuple-element.14.refs_2_, ...), custom_call_target="tpu_custom_call" | custom-call | tf_op jit(solution)/shard_map/pallas_call | solution.py:635

commit v5 on v4

--- a/solution.py
+++ b/solution.py
@@ -23,6 +23,7 @@
 SPAN = 2 * COUT
 MIX = 2
 ORDER = (2, 0, 1)
+UP = (0, 1)
 LON_ALL = 16
 MESH = pl.DeviceIdType.MESH
 F32 = jnp.float32
@@ -365,6 +366,9 @@
     xb_in,
     y_out,
     y_in,
+    mix_y_in,
+    mix_out_x,
+    mix_x_in,
     far,
     near,
     final,
@@ -374,6 +378,7 @@
     far_sem,
     near_sem,
     final_sem,
+    mix_sem,
 ):
     z_count, y_count = lat_count // 4, lon_count // 2
     far_count, near_count = z_plan(z_count)
@@ -414,7 +419,7 @@
     barrier = pltpu.get_barrier_semaphore()
     up, down, left, right = partners = halo_partners(lat, lon, lat_count, lon_count)
     greeted = [(a, b) for a in (up, down) for b in (left, lon, right)] + [(lat, left), (lat, right)]
-    greeted += [partner, at_x(1), at_x(-1)]
+    greeted += [partner, at_x(1), at_x(2), at_x(-1)]
     greeted += [at_y(step) for step in range(1, y_count)]
     far_all = sorted({step % z_count for base in far_steps for step in (base, -base)})
     near_all = sorted({step % z_count for base in near_steps for step in (base, -base)})
@@ -440,12 +445,49 @@
     def core_start(part):
         fetch(sums.at[1 - core, part], core_in.at[part], core_sem.at[0, part], core_sem.at[1, part], partner)
 
-    half = CIN // 4
-
-    def x_first(part):
+    half = y_count // 2
+    y_steps = sorted(range(1, y_count), key=lambda step: -min(step, y_count - step))
+
+    def core_end(part):
         await_bytes(core_in.at[part], core_sem.at[1, part])
         merged = sums[core, part].astype(F32) + core_in[part].astype(F32)
         x_out[part] = merged.astype(BF16).reshape(x_out.shape[1:])
+
+    def mix_first():
+        core_end(MIX)
+        for step in y_steps:
+            fetch(
+                x_out.at[MIX, :, lax.rem(y + step, y_count)],
+                mix_y_in.at[step - 1],
+                mix_sem.at[0],
+                mix_sem.at[1],
+                at_y(step),
+            )
+
+    def mix_second():
+        await_bytes(mix_y_in, mix_sem.at[1])
+        total = x_out[MIX, :, y].astype(F32)
+        for step in range(y_count - 1):
+            total = total + mix_y_in[step].astype(F32)
+        mix_out_x[...] = total.astype(BF16)
+        for step in (2, 1, 3):
+            fetch(
+                mix_out_x.at[lax.rem(x + step, 4)],
+                mix_x_in.at[step - 1],
+                mix_sem.at[2],
+                mix_sem.at[3],
+                at_x(step),
+            )
+
+    def mix_third():
+        await_bytes(mix_x_in, mix_sem.at[3])
+        total = mix_out_x[x].astype(F32)
+        for step in range(3):
+            total = total + mix_x_in[step].astype(F32)
+        far_send(MIX, total)
+
+    def x_first(part):
+        core_end(part)
         across = lax.rem(x + 2, 4)
         for side, step in ((0, 1), (1, -1)):
             fetch(
@@ -475,8 +517,8 @@
         for side in range(2):
             await_bytes(xb_in.at[part, side], x_sem.at[3, part, side])
         merged = x_out[part, x].astype(F32) + xb_in[part, 0].astype(F32) + xb_in[part, 1].astype(F32)
-        y_out[part] = merged.astype(BF16).reshape(y_out.shape[1:])
-        for step in range(1, y_count):
+        y_out[part] = merged.astype(BF16)
+        for step in y_steps:
             fetch(
                 y_out.at[part, lax.rem(y + step, y_count)],
                 y_in.at[part, step - 1],
@@ -492,6 +534,9 @@
         total = y_out[part, y].astype(F32)
         for step in range(y_count - 1):
             total = total + y_in[part, step].astype(F32)
+        far_send(part, total)
+
+    def far_send(part, total):
         far[part, far_at] = total.astype(BF16)
         for step in far_steps:
             fetch(far.at[part, far_at], far.at[part, far_at], far_sem.at[0, part], far_sem.at[1, part], at_z(step, x_hi))
@@ -537,26 +582,35 @@
     backward_part(grid, mix_kernel, slope, outside, pre_grad)
     up_part_sums(grid, pre_grad, 0, sums)
     core_start(0)
-    x_first(MIX)
+    mix_first()
     up_part_sums(grid, pre_grad, 1, sums)
     core_start(1)
     x_first(0)
     x_first(1)
     section_part(act_patches, mix_kernel, staged, out_wide, section)
-    for part in ORDER:
+    for part in UP:
         x_second(part)
     input_part(pre_grad, up_kernel, act, input_grad)
-    for stage in (y_start, far_start, near_start, final_start):
+    for part in UP:
+        y_start(part)
+    mix_second()
+    mix_third()
+    for part in UP:
+        far_start(part)
+    for stage in (near_start, final_start):
         for part in ORDER:
             stage(part)
     for copy in halo:
         copy.wait_send()
-    for part in range(PARTS):
-        await_bytes(core_in.at[part], core_sem.at[0, part])
+    await_bytes(mix_y_in, mix_sem.at[0])
+    await_bytes(mix_x_in, mix_sem.at[2])
+    for part in UP:
         for side in range(2):
             await_bytes(xa_in.at[part, side], x_sem.at[0, part, side])
             await_bytes(xb_in.at[part, side], x_sem.at[2, part, side])
         await_bytes(y_in.at[part], y_sem.at[0, part])
+    for part in range(PARTS):
+        await_bytes(core_in.at[part], core_sem.at[0, part])
         await_bytes(far.at[part, pl.ds(0, far_count - 1)], far_sem.at[0, part])
         await_bytes(near.at[part, pl.ds(0, 2 * near_count - 1)], near_sem.at[0, part])
         await_bytes(final.at[part, 0], final_sem.at[0, part])
@@ -613,20 +667,24 @@
             pltpu.VMEM((4 * CELLS, COUT), F32),
             pltpu.VMEM((2, PARTS, 2, CIN, SPAN), BF16),
             pltpu.VMEM((PARTS, 2, CIN, SPAN), BF16),
-            pltpu.VMEM((PARTS, 4, CIN // 2, SPAN), BF16),
-            pltpu.VMEM((PARTS, 2, CIN // 4, SPAN), BF16),
-            pltpu.VMEM((PARTS, 2, CIN // 2, SPAN), BF16),
-            pltpu.VMEM((PARTS, y_count, 16, SPAN), BF16),
-            pltpu.VMEM((PARTS, y_count - 1, 16, SPAN), BF16),
+            pltpu.VMEM((PARTS, 4, y_count, 16, SPAN), BF16),
+            pltpu.VMEM((2, 2, y_count // 2, 16, SPAN), BF16),
+            pltpu.VMEM((2, 2, y_count, 16, SPAN), BF16),
+            pltpu.VMEM((2, y_count, 16, SPAN), BF16),
+            pltpu.VMEM((2, y_count - 1, 16, SPAN), BF16),
+            pltpu.VMEM((y_count - 1, 4, 16, SPAN), BF16),
+            pltpu.VMEM((4, 16, SPAN), BF16),
+            pltpu.VMEM((3, 16, SPAN), BF16),
             pltpu.VMEM((PARTS, far_count, 16, SPAN), BF16),
             pltpu.VMEM((PARTS, 2 * near_count, 16, SPAN), BF16),
             pltpu.VMEM((PARTS, 2, 2, 16, SPAN), F32),
             dma((2, PARTS)),
-            dma((4, PARTS, 2)),
+            dma((4, 2, 2)),
+            dma((2, 2)),
             dma((2, PARTS)),
             dma((2, PARTS)),
             dma((2, PARTS)),
-            dma((2, PARTS)),
+            dma((4,)),
         ],
         compiler_params=pltpu.CompilerParams(
             collective_id=0, has_side_effects=True, vmem_limit_bytes=56 * 2**20

time: 55.9 us -> 55 us (0.984)
  Pallas kernels: 55.1 us -> 54.2 us
    pallas_call x1, Pallas kernels: 53.3 us -> 52.4 us  [shards(): pl.pallas_call(functools.partial(section_kernel, lat_count, lon_count, 1....]
where the time goes in v5:
time: 55 us; the launch traced here: 54.9 us
  Pallas kernels  54.2 us (99%)
  between operations  0.64 us (1%)
    pallas_call x1, Pallas kernels, shards(): pl.pallas_call(functools.partial(section_kernel, lat_count, lon_count, 1....  52.4 us
    pallas_call x1, Pallas kernels, shards(): pl.pallas_call(write_kernel, out_shape=tuple((jax.ShapeDtypeStruct(result...  1.79 us

profile of v5, /device:TPU:1, one launch (start us, length us, event | category | flops | bytes accessed | tf_op | source)
XLA Modules:
  0.0 54.9 jit_solution(15701003444002547394)
XLA Ops:
  0.6 52.4 %shard_map.93 = (bf16[512,128]{1,0:T(8,128)(2,1)}, f32[128,256]{1,0:T(8,128)}, f32[4,4,16,128]{3,2,1,0:T(8,128)}, f32[9,8,128]{2,1,0:T(8,128)}) custom-call(s32[128,256]{1,0:T(8,128)} %bitcast.13, s32[64,16]{1,0:T(8,128)} %bitcast.15, bf16[512,128]{1,0:T(8,128)(2,1)} %bitcast.14, bf16[16,256,128]{2,1,0:T(8,128)(2,1)} %bitcast.11, f32[1,128]{1,0:T(1,128)} %bitcast.16, ...), custom_call_target="tpu_custom_call" | custom-call | tf_op jit(solution)/shard_map/pallas_call | solution.py:640
  53.1 1.8 %shard_map.94 = (bf16[512,128]{1,0:T(8,128)(2,1)}, f32[128,256]{1,0:T(8,128)}, f32[4,4,16,128]{3,2,1,0:T(8,128)}, f32[9,8,128]{2,1,0:T(8,128)}) custom-call(bf16[512,128]{1,0:T(8,128)(2,1)} %get-tuple-element.12.refs_0_, f32[128,256]{1,0:T(8,128)} %get-tuple-element.13.refs_1_, f32[4,4,16,128]{3,2,1,0:T(8,128)} %get-tuple-element.14.refs_2_, ...), custom_call_target="tpu_custom_call" | custom-call | tf_op jit(solution)/shard_map/pallas_call | solution.py:693

commit v6 on v5

--- a/solution.py
+++ b/solution.py
@@ -434,7 +434,7 @@
     halo = halo_copies(
         partners, lat, lon, row_out, col_out, corner_out, row_in, col_in, corner_in, halo_send, halo_recv
     )
-    for copy in halo:
+    for copy in reversed(halo):
         copy.start()
     for load in loads[3:]:
         load.wait()
@@ -587,16 +587,16 @@
     core_start(1)
     x_first(0)
     x_first(1)
-    section_part(act_patches, mix_kernel, staged, out_wide, section)
     for part in UP:
         x_second(part)
-    input_part(pre_grad, up_kernel, act, input_grad)
     for part in UP:
         y_start(part)
     mix_second()
+    section_part(act_patches, mix_kernel, staged, out_wide, section)
     mix_third()
     for part in UP:
         far_start(part)
+    input_part(pre_grad, up_kernel, act, input_grad)
     for stage in (near_start, final_start):
         for part in ORDER:
             stage(part)

time: 55 us -> 54.6 us (level)
  no operation moved by 1% of the time
where the time goes in v6:
time: 54.6 us; the launch traced here: 54.4 us
  Pallas kernels  53.8 us (99%)
  between operations  0.64 us (1%)
    pallas_call x1, Pallas kernels, shards(): pl.pallas_call(functools.partial(section_kernel, lat_count, lon_count, 1....  52 us
    pallas_call x1, Pallas kernels, shards(): pl.pallas_call(write_kernel, out_shape=tuple((jax.ShapeDtypeStruct(result...  1.79 us

profile of v6, /device:TPU:1, one launch (start us, length us, event | category | flops | bytes accessed | tf_op | source)
XLA Modules:
  0.0 54.4 jit_solution(2035597946394304470)
XLA Ops:
  0.6 52.0 %shard_map.93 = (bf16[512,128]{1,0:T(8,128)(2,1)}, f32[128,256]{1,0:T(8,128)}, f32[4,4,16,128]{3,2,1,0:T(8,128)}, f32[9,8,128]{2,1,0:T(8,128)}) custom-call(s32[128,256]{1,0:T(8,128)} %bitcast.13, s32[64,16]{1,0:T(8,128)} %bitcast.15, bf16[512,128]{1,0:T(8,128)(2,1)} %bitcast.14, bf16[16,256,128]{2,1,0:T(8,128)(2,1)} %bitcast.11, f32[1,128]{1,0:T(1,128)} %bitcast.16, ...), custom_call_target="tpu_custom_call" | custom-call | tf_op jit(solution)/shard_map/pallas_call | solution.py:640
  52.6 1.8 %shard_map.94 = (bf16[512,128]{1,0:T(8,128)(2,1)}, f32[128,256]{1,0:T(8,128)}, f32[4,4,16,128]{3,2,1,0:T(8,128)}, f32[9,8,128]{2,1,0:T(8,128)}) custom-call(bf16[512,128]{1,0:T(8,128)(2,1)} %get-tuple-element.12.refs_0_, f32[128,256]{1,0:T(8,128)} %get-tuple-element.13.refs_1_, f32[4,4,16,128]{3,2,1,0:T(8,128)} %get-tuple-element.14.refs_2_, ...), custom_call_target="tpu_custom_call" | custom-call | tf_op jit(solution)/shard_map/pallas_call | solution.py:693

commit v7 on v6

--- a/solution.py
+++ b/solution.py
@@ -413,9 +413,6 @@
             )
         )
     ]
-    for load in loads:
-        load.start()
-
     barrier = pltpu.get_barrier_semaphore()
     up, down, left, right = partners = halo_partners(lat, lon, lat_count, lon_count)
     greeted = [(a, b) for a in (up, down) for b in (left, lon, right)] + [(lat, left), (lat, right)]
@@ -427,6 +424,8 @@
     greeted += [at_z(step, 1 - x_hi) for step in [0] + near_all]
     for to in greeted:
         pl.semaphore_signal(barrier, inc=1, device_id=to, device_id_type=MESH)
+    for load in loads:
+        load.start()
     for load in loads[:3]:
         load.wait()
     halo_fill(codes, exps, cot, grid, own, cot_wide, row_out, col_out, corner_out)
@@ -619,8 +618,11 @@
 
 
 def write_kernel(*refs):
-    for i in range(4):
-        refs[4 + i][...] = refs[i][...]
+    copies = [pltpu.make_async_copy(refs[i], refs[4 + i], refs[8].at[i]) for i in range(4)]
+    for copy in copies:
+        copy.start()
+    for copy in copies:
+        copy.wait()
 
 
 def shards(elem_codes, block_exps, up_kernel, up_bias, mix_kernel, cotangent):
@@ -640,10 +642,10 @@
     results = pl.pallas_call(
         functools.partial(section_kernel, lat_count, lon_count, 1.0 / math.sqrt(out_cells)),
         out_shape=(
-            jax.ShapeDtypeStruct((4 * CELLS, COUT), BF16),
-            jax.ShapeDtypeStruct((CELLS, CIN), F32),
-            jax.ShapeDtypeStruct((4, 4, LON_ALL, COUT), F32),
-            jax.ShapeDtypeStruct((9, 8, COUT), F32),
+            pltpu.VMEM((4 * CELLS, COUT), BF16),
+            pltpu.VMEM((CELLS, CIN), F32),
+            pltpu.VMEM((4, 4, LON_ALL, COUT), F32),
+            pltpu.VMEM((9, 8, COUT), F32),
         ),
         in_specs=[pl.BlockSpec(memory_space=pltpu.HBM)] * 6,
         out_specs=[pl.BlockSpec(memory_space=pltpu.VMEM)] * 4,
@@ -687,15 +689,16 @@
             dma((4,)),
         ],
         compiler_params=pltpu.CompilerParams(
-            collective_id=0, has_side_effects=True, vmem_limit_bytes=56 * 2**20
+            collective_id=0, has_side_effects=True, vmem_limit_bytes=40 * 2**20
         ),
-    )(*operands)
+    )(*[pltpu.with_memory_space_constraint(operand, pltpu.HBM) for operand in operands])
     section, input_grad, up_part, mix_part = pl.pallas_call(
         write_kernel,
         out_shape=tuple(jax.ShapeDtypeStruct(result.shape, result.dtype) for result in results),
         in_specs=[pl.BlockSpec(memory_space=pltpu.VMEM)] * 4,
-        out_specs=[pl.BlockSpec(memory_space=pltpu.VMEM)] * 4,
-        compiler_params=pltpu.CompilerParams(vmem_limit_bytes=56 * 2**20),
+        out_specs=[pl.BlockSpec(memory_space=pltpu.HBM)] * 4,
+        scratch_shapes=[dma((4,))],
+        compiler_params=pltpu.CompilerParams(vmem_limit_bytes=8 * 2**20),
     )(*results)
     return (
         section.reshape(2 * ROWS, 2 * COLS, COUT),

time: 54.6 us -> 52.8 us (0.967)
  Pallas kernels: 53.8 us -> 52 us
    pallas_call x1, Pallas kernels: 1.79 us -> 0.78 us  [shards(): pl.pallas_call(write_kernel, out_shape=tuple((jax.ShapeDtypeStruct(result...]
    pallas_call x1, Pallas kernels: 52 us -> 51.2 us  [shards(): pl.pallas_call(functools.partial(section_kernel, lat_count, lon_count, 1....]
where the time goes in v7:
time: 52.8 us; the launch traced here: 52.6 us
  Pallas kernels  52 us (98%)
  between operations  0.64 us (1%)
    pallas_call x1, Pallas kernels, shards(): pl.pallas_call(functools.partial(section_kernel, lat_count, lon_count, 1....  51.2 us

profile of v7, /device:TPU:1, one launch (start us, length us, event | category | flops | bytes accessed | tf_op | source)
XLA Modules:
  0.0 52.6 jit_solution(6312491533005705817)
XLA Ops:
  0.6 51.2 %shard_map.93 = (bf16[512,128]{1,0:T(8,128)(2,1)S(1)}, f32[128,256]{1,0:T(8,128)S(1)}, f32[4,4,16,128]{3,2,1,0:T(8,128)S(1)}, f32[9,8,128]{2,1,0:T(8,128)S(1)}) custom-call(s32[128,256]{1,0:T(8,128)} %bitcast.13, s32[64,16]{1,0:T(8,128)} %bitcast.15, bf16[512,128]{1,0:T(8,128)(2,1)} %bitcast.14, bf16[16,256,128]{2,1,0:T(8,128)(2,1)} %bitcast.11, ...), custom_call_target="tpu_custom_call" | custom-call | tf_op jit(solution)/shard_map/pallas_call | solution.py:642
  51.8 0.8 %shard_map.94 = (bf16[512,128]{1,0:T(8,128)(2,1)}, f32[128,256]{1,0:T(8,128)}, f32[4,4,16,128]{3,2,1,0:T(8,128)}, f32[9,8,128]{2,1,0:T(8,128)}) custom-call(bf16[512,128]{1,0:T(8,128)(2,1)S(1)} %get-tuple-element.12.refs_0_, f32[128,256]{1,0:T(8,128)S(1)} %get-tuple-element.13.refs_1_, f32[4,4,16,128]{3,2,1,0:T(8,128)S(1)} %get-tuple-element.14.refs_2_, ...), custom_call_target="tpu_custom_call" | custom-call | tf_op jit(solution)/shard_map/pallas_call | solution.py:695

commit v8 on v7

--- a/solution.py
+++ b/solution.py
@@ -22,7 +22,8 @@
 PARTS = 3
 SPAN = 2 * COUT
 MIX = 2
-ORDER = (2, 0, 1)
+MIX_TAPS = (5, 4)
+MIX_ROWS = 48
 UP = (0, 1)
 LON_ALL = 16
 MESH = pl.DeviceIdType.MESH
@@ -185,10 +186,6 @@
     return lax.rem(cell, PITCH) < COLS
 
 
-def merge_slots(even, odd):
-    return jnp.concatenate([even, odd], axis=1).reshape(CIN, COUT).astype(BF16)
-
-
 def forward_part(lat, lat_count, grid, up_kernel, bias, act):
     windows = [window(grid, dr * PITCH + dc, OUTER, 0, 2).astype(BF16) for dr, dc in OFFSETS]
     forward = jnp.concatenate(
@@ -218,7 +215,7 @@
     return sigmoid * (1.0 + plain * (1.0 - sigmoid)), outside
 
 
-def mix_part_sums(grid, act_patches, sums):
+def mix_part_sums(grid, act_patches, mix_sums):
     cot_own = window(grid, PITCH + 1, INNER, 2, TALL)
     cot_own = jnp.where(inner_mask(4 * COUT), cot_own, 0.0).astype(BF16)
     cot_stacked = jnp.concatenate([cot_own[:, i * COUT : (i + 1) * COUT] for i in range(4)], axis=0)
@@ -226,16 +223,13 @@
         act_patches, cot_stacked, (((0,), (0,)), ((), ())), preferred_element_type=F32
     )
     empty = jnp.zeros((LON_ALL, 8, COUT), F32)
-    for w in range(4):
-        slots = [empty] * 4
-        for slot in range(4):
-            tap = slot * 4 + w
-            if tap < 9:
-                slots[slot] = mix_sum[tap * COUT : (tap + 1) * COUT].reshape(LON_ALL, 8, COUT)
-        for i in range(2):
-            sums[w // 2, MIX, w % 2, :, i * COUT : (i + 1) * COUT] = merge_slots(
-                slots[2 * i], slots[2 * i + 1]
-            )
+    tap = 0
+    for core, count in enumerate(MIX_TAPS):
+        rows = [empty] * (MIX_ROWS // 8)
+        for i in range(count):
+            rows[i] = mix_sum[tap * COUT : (tap + 1) * COUT].reshape(LON_ALL, 8, COUT)
+            tap += 1
+        mix_sums[core] = jnp.concatenate(rows, axis=1).astype(BF16).reshape(mix_sums.shape[1:])
 
 
 def backward_part(grid, mix_kernel, slope, outside, pre_grad):
@@ -366,9 +360,15 @@
     xb_in,
     y_out,
     y_in,
+    mix_sums,
+    mix_core_in,
+    mix_y_out,
     mix_y_in,
-    mix_out_x,
+    mix_x_out,
     mix_x_in,
+    mix_far,
+    mix_near,
+    mix_final,
     far,
     near,
     final,
@@ -453,10 +453,11 @@
         x_out[part] = merged.astype(BF16).reshape(x_out.shape[1:])
 
     def mix_first():
-        core_end(MIX)
+        await_bytes(mix_core_in, core_sem.at[1, MIX])
+        mix_y_out[...] = (mix_sums[core].astype(F32) + mix_core_in[...].astype(F32)).astype(BF16)
         for step in y_steps:
             fetch(
-                x_out.at[MIX, :, lax.rem(y + step, y_count)],
+                mix_y_out.at[:, lax.rem(y + step, y_count)],
                 mix_y_in.at[step - 1],
                 mix_sem.at[0],
                 mix_sem.at[1],
@@ -465,25 +466,48 @@
 
     def mix_second():
         await_bytes(mix_y_in, mix_sem.at[1])
-        total = x_out[MIX, :, y].astype(F32)
+        total = mix_y_out[:, y].astype(F32)
         for step in range(y_count - 1):
             total = total + mix_y_in[step].astype(F32)
-        mix_out_x[...] = total.astype(BF16)
+        mix_x_out[...] = total.astype(BF16)
         for step in (2, 1, 3):
             fetch(
-                mix_out_x.at[lax.rem(x + step, 4)],
-                mix_x_in.at[step - 1],
-                mix_sem.at[2],
-                mix_sem.at[3],
-                at_x(step),
+                mix_x_out.at[lax.rem(x + step, 2)], mix_x_in.at[x], mix_sem.at[2], mix_sem.at[3], at_x(step)
             )
+        mix_x_in[x] = mix_x_out[x_lo]
+
+    def summed(ref, count):
+        total = ref[0].astype(F32)
+        for i in range(1, count):
+            total = total + ref[i].astype(F32)
+        return total
 
     def mix_third():
-        await_bytes(mix_x_in, mix_sem.at[3])
-        total = mix_out_x[x].astype(F32)
-        for step in range(3):
-            total = total + mix_x_in[step].astype(F32)
-        far_send(MIX, total)
+        await_bytes(mix_x_in.at[pl.ds(0, 3)], mix_sem.at[3])
+        mix_far[far_at] = summed(mix_x_in, 4).astype(BF16)
+        for step in far_steps:
+            fetch(mix_far.at[far_at], mix_far.at[far_at], far_sem.at[0, MIX], far_sem.at[1, MIX], at_z(step, x_hi))
+
+    def mix_fourth():
+        await_bytes(mix_far.at[pl.ds(0, far_count - 1)], far_sem.at[1, MIX])
+        mix_near[near_at] = summed(mix_far, far_count).astype(BF16)
+        for step in near_steps:
+            fetch(
+                mix_near.at[near_at], mix_near.at[near_at], near_sem.at[0, MIX], near_sem.at[1, MIX], at_z(step, x_hi)
+            )
+
+    def mix_fifth():
+        await_bytes(mix_near.at[pl.ds(0, near_count - 1)], near_sem.at[1, MIX])
+        mix_final[core] = summed(mix_near, near_count) * scale
+        fetch(mix_final.at[core], mix_final.at[core], final_sem.at[0, MIX], final_sem.at[1, MIX], partner)
+
+    def mix_finish():
+        await_bytes(mix_final.at[0], final_sem.at[1, MIX])
+        tap = 0
+        for owner, count in enumerate(MIX_TAPS):
+            for i in range(count):
+                mix_out[tap] = mix_final[owner, i * 8 : i * 8 + 8, :]
+                tap += 1
 
     def x_first(part):
         core_end(part)
@@ -565,25 +589,18 @@
         await_bytes(final.at[part, 0], final_sem.at[1, part])
         for w in range(4):
             for i in range(2):
-                piece = final[part, w // 2, w % 2, :, i * COUT : (i + 1) * COUT]
-                if part != MIX:
-                    up_out[w, 2 * part + i] = piece
-                    continue
-                for slot in range(2):
-                    tap = (2 * i + slot) * 4 + w
-                    if tap < 9:
-                        mix_out[tap] = piece[slot * 8 : slot * 8 + 8]
+                up_out[w, 2 * part + i] = final[part, w // 2, w % 2, :, i * COUT : (i + 1) * COUT]
 
     slope, outside = forward_part(lat, lat_count, grid, up_kernel, bias, act)
     act_patches = patches(positions(act, INNER, 0), False)
-    mix_part_sums(grid, act_patches, sums)
-    core_start(MIX)
+    mix_part_sums(grid, act_patches, mix_sums)
+    fetch(mix_sums.at[1 - core], mix_core_in, core_sem.at[0, MIX], core_sem.at[1, MIX], partner)
     backward_part(grid, mix_kernel, slope, outside, pre_grad)
     up_part_sums(grid, pre_grad, 0, sums)
     core_start(0)
-    mix_first()
     up_part_sums(grid, pre_grad, 1, sums)
     core_start(1)
+    mix_first()
     x_first(0)
     x_first(1)
     for part in UP:
@@ -596,24 +613,31 @@
     for part in UP:
         far_start(part)
     input_part(pre_grad, up_kernel, act, input_grad)
-    for stage in (near_start, final_start):
-        for part in ORDER:
-            stage(part)
+    mix_fourth()
+    for part in UP:
+        near_start(part)
+    mix_fifth()
+    for part in UP:
+        final_start(part)
+    mix_finish()
     for copy in halo:
         copy.wait_send()
     await_bytes(mix_y_in, mix_sem.at[0])
-    await_bytes(mix_x_in, mix_sem.at[2])
+    await_bytes(mix_x_in.at[pl.ds(0, 3)], mix_sem.at[2])
+    await_bytes(mix_core_in, core_sem.at[0, MIX])
+    await_bytes(mix_far.at[pl.ds(0, far_count - 1)], far_sem.at[0, MIX])
+    await_bytes(mix_near.at[pl.ds(0, near_count - 1)], near_sem.at[0, MIX])
+    await_bytes(mix_final.at[0], final_sem.at[0, MIX])
     for part in UP:
         for side in range(2):
             await_bytes(xa_in.at[part, side], x_sem.at[0, part, side])
             await_bytes(xb_in.at[part, side], x_sem.at[2, part, side])
         await_bytes(y_in.at[part], y_sem.at[0, part])
-    for part in range(PARTS):
         await_bytes(core_in.at[part], core_sem.at[0, part])
         await_bytes(far.at[part, pl.ds(0, far_count - 1)], far_sem.at[0, part])
         await_bytes(near.at[part, pl.ds(0, 2 * near_count - 1)], near_sem.at[0, part])
         await_bytes(final.at[part, 0], final_sem.at[0, part])
-    for part in ORDER:
+    for part in UP:
         finish(part)
 
 
@@ -667,19 +691,25 @@
             pltpu.VMEM((4, FLAT, COUT), F32),
             pltpu.VMEM((4 * INNER, COUT), F32),
             pltpu.VMEM((4 * CELLS, COUT), F32),
-            pltpu.VMEM((2, PARTS, 2, CIN, SPAN), BF16),
-            pltpu.VMEM((PARTS, 2, CIN, SPAN), BF16),
-            pltpu.VMEM((PARTS, 4, y_count, 16, SPAN), BF16),
+            pltpu.VMEM((2, 2, 2, CIN, SPAN), BF16),
+            pltpu.VMEM((2, 2, CIN, SPAN), BF16),
+            pltpu.VMEM((2, 4, y_count, 16, SPAN), BF16),
             pltpu.VMEM((2, 2, y_count // 2, 16, SPAN), BF16),
             pltpu.VMEM((2, 2, y_count, 16, SPAN), BF16),
             pltpu.VMEM((2, y_count, 16, SPAN), BF16),
             pltpu.VMEM((2, y_count - 1, 16, SPAN), BF16),
-            pltpu.VMEM((y_count - 1, 4, 16, SPAN), BF16),
-            pltpu.VMEM((4, 16, SPAN), BF16),
-            pltpu.VMEM((3, 16, SPAN), BF16),
-            pltpu.VMEM((PARTS, far_count, 16, SPAN), BF16),
-            pltpu.VMEM((PARTS, 2 * near_count, 16, SPAN), BF16),
-            pltpu.VMEM((PARTS, 2, 2, 16, SPAN), F32),
+            pltpu.VMEM((2, 2, y_count, MIX_ROWS, COUT), BF16),
+            pltpu.VMEM((2, y_count, MIX_ROWS, COUT), BF16),
+            pltpu.VMEM((2, y_count, MIX_ROWS, COUT), BF16),
+            pltpu.VMEM((y_count - 1, 2, MIX_ROWS, COUT), BF16),
+            pltpu.VMEM((2, MIX_ROWS, COUT), BF16),
+            pltpu.VMEM((4, MIX_ROWS, COUT), BF16),
+            pltpu.VMEM((far_count, MIX_ROWS, COUT), BF16),
+            pltpu.VMEM((near_count, MIX_ROWS, COUT), BF16),
+            pltpu.VMEM((2, MIX_ROWS, COUT), F32),
+            pltpu.VMEM((2, far_count, 16, SPAN), BF16),
+            pltpu.VMEM((2, 2 * near_count, 16, SPAN), BF16),
+            pltpu.VMEM((2, 2, 2, 16, SPAN), F32),
             dma((2, PARTS)),
             dma((4, 2, 2)),
             dma((2, 2)),

time: 52.8 us -> 52.4 us (level)
  no operation moved by 1% of the time
where the time goes in v8:
time: 52.4 us; the launch traced here: 52.2 us
  Pallas kernels  51.6 us (98%)
  between operations  0.64 us (1%)
    pallas_call x1, Pallas kernels, shards(): pl.pallas_call(functools.partial(section_kernel, lat_count, lon_count, 1....  50.8 us

profile of v8, /device:TPU:1, one launch (start us, length us, event | category | flops | bytes accessed | tf_op | source)
XLA Modules:
  0.0 52.2 jit_solution(392822437419597298)
XLA Ops:
  0.6 50.8 %shard_map.93 = (bf16[512,128]{1,0:T(8,128)(2,1)S(1)}, f32[128,256]{1,0:T(8,128)S(1)}, f32[4,4,16,128]{3,2,1,0:T(8,128)S(1)}, f32[9,8,128]{2,1,0:T(8,128)S(1)}) custom-call(s32[128,256]{1,0:T(8,128)} %bitcast.13, s32[64,16]{1,0:T(8,128)} %bitcast.15, bf16[512,128]{1,0:T(8,128)(2,1)} %bitcast.14, bf16[16,256,128]{2,1,0:T(8,128)(2,1)} %bitcast.11, ...), custom_call_target="tpu_custom_call" | custom-call | tf_op jit(solution)/shard_map/pallas_call | solution.py:666
  51.5 0.8 %shard_map.94 = (bf16[512,128]{1,0:T(8,128)(2,1)}, f32[128,256]{1,0:T(8,128)}, f32[4,4,16,128]{3,2,1,0:T(8,128)}, f32[9,8,128]{2,1,0:T(8,128)}) custom-call(bf16[512,128]{1,0:T(8,128)(2,1)S(1)} %get-tuple-element.12.refs_0_, f32[128,256]{1,0:T(8,128)S(1)} %get-tuple-element.13.refs_1_, f32[4,4,16,128]{3,2,1,0:T(8,128)S(1)} %get-tuple-element.14.refs_2_, ...), custom_call_target="tpu_custom_call" | custom-call | tf_op jit(solution)/shard_map/pallas_call | solution.py:725

commit v9 on v8

--- a/solution.py
+++ b/solution.py
@@ -19,12 +19,12 @@
 FLAT = 192
 OUTER = 176
 INNER = ROWS * PITCH
-PARTS = 3
-SPAN = 2 * COUT
-MIX = 2
+PARTS = 5
+SPAN = COUT
+MIX = 4
 MIX_TAPS = (5, 4)
 MIX_ROWS = 48
-UP = (0, 1)
+UP = (0, 1, 2, 3)
 LON_ALL = 16
 MESH = pl.DeviceIdType.MESH
 F32 = jnp.float32
@@ -121,20 +121,23 @@
     ]
 
 
-def halo_place(lat, lat_count, grid, row_in, col_in, corner_in):
+def halo_place(copies, lat, lat_count, grid, row_in, col_in, corner_in):
     above = (lat > 0).astype(F32)
     below = (lat < lat_count - 1).astype(F32)
     for side, (r, keep) in enumerate(((0, above), (ROWS + 1, below))):
+        copies[side].wait_recv()
         at = r * PITCH + 1
         for i in range(TALL // 2):
             part = row_in[side, i].astype(F32) * keep
             grid[2 * i, at : at + COLS, :] = part[:COLS]
             grid[2 * i + 1, at : at + COLS, :] = part[COLS:]
     for side, c in enumerate((0, COLS + 1)):
+        copies[2 + side].wait_recv()
         for i in range(TALL):
             grid[i, pl.ds(PITCH + c, ROWS, stride=PITCH), :] = col_in[side, i].astype(F32)
     places = ((0, 0, above), (0, COLS + 1, above), (ROWS + 1, 0, below), (ROWS + 1, COLS + 1, below))
     for corner, (r, c, keep) in enumerate(places):
+        copies[4 + corner].wait_recv()
         cell = r * PITCH + c
         for i in range(TALL):
             grid[i, cell : cell + 1, :] = corner_in[corner, i : i + 1, :] * keep
@@ -259,7 +262,9 @@
             preferred_element_type=F32,
         ).astype(BF16)
         for pr in range(2):
-            sums[dr, dc, pr] = up_sum[:, pr * SPAN : (pr + 1) * SPAN]
+            for pc in range(2):
+                at = (2 * pr + pc) * COUT
+                sums[dr, 2 * dc + pc, pr] = up_sum[:, at : at + COUT]
 
 
 def section_part(act_patches, mix_kernel, staged, out_wide, section):
@@ -437,9 +442,7 @@
         copy.start()
     for load in loads[3:]:
         load.wait()
-    for copy in halo:
-        copy.wait_recv()
-    halo_place(lat, lat_count, grid, row_in, col_in, corner_in)
+    halo_place(halo, lat, lat_count, grid, row_in, col_in, corner_in)
 
     def core_start(part):
         fetch(sums.at[1 - core, part], core_in.at[part], core_sem.at[0, part], core_sem.at[1, part], partner)
@@ -588,21 +591,20 @@
     def finish(part):
         await_bytes(final.at[part, 0], final_sem.at[1, part])
         for w in range(4):
-            for i in range(2):
-                up_out[w, 2 * part + i] = final[part, w // 2, w % 2, :, i * COUT : (i + 1) * COUT]
+            up_out[w, part] = final[part, w // 2, w % 2]
 
     slope, outside = forward_part(lat, lat_count, grid, up_kernel, bias, act)
     act_patches = patches(positions(act, INNER, 0), False)
     mix_part_sums(grid, act_patches, mix_sums)
     fetch(mix_sums.at[1 - core], mix_core_in, core_sem.at[0, MIX], core_sem.at[1, MIX], partner)
     backward_part(grid, mix_kernel, slope, outside, pre_grad)
-    up_part_sums(grid, pre_grad, 0, sums)
-    core_start(0)
-    up_part_sums(grid, pre_grad, 1, sums)
-    core_start(1)
+    for dc in range(2):
+        up_part_sums(grid, pre_grad, dc, sums)
+        for pc in range(2):
+            core_start(2 * dc + pc)
     mix_first()
-    x_first(0)
-    x_first(1)
+    for part in UP:
+        x_first(part)
     for part in UP:
         x_second(part)
     for part in UP:
@@ -691,13 +693,13 @@
             pltpu.VMEM((4, FLAT, COUT), F32),
             pltpu.VMEM((4 * INNER, COUT), F32),
             pltpu.VMEM((4 * CELLS, COUT), F32),
-            pltpu.VMEM((2, 2, 2, CIN, SPAN), BF16),
-            pltpu.VMEM((2, 2, CIN, SPAN), BF16),
-            pltpu.VMEM((2, 4, y_count, 16, SPAN), BF16),
-            pltpu.VMEM((2, 2, y_count // 2, 16, SPAN), BF16),
-            pltpu.VMEM((2, 2, y_count, 16, SPAN), BF16),
-            pltpu.VMEM((2, y_count, 16, SPAN), BF16),
-            pltpu.VMEM((2, y_count - 1, 16, SPAN), BF16),
+            pltpu.VMEM((2, len(UP), 2, CIN, SPAN), BF16),
+            pltpu.VMEM((len(UP), 2, CIN, SPAN), BF16),
+            pltpu.VMEM((len(UP), 4, y_count, 16, SPAN), BF16),
+            pltpu.VMEM((len(UP), 2, y_count // 2, 16, SPAN), BF16),
+            pltpu.VMEM((len(UP), 2, y_count, 16, SPAN), BF16),
+            pltpu.VMEM((len(UP), y_count, 16, SPAN), BF16),
+            pltpu.VMEM((len(UP), y_count - 1, 16, SPAN), BF16),
             pltpu.VMEM((2, 2, y_count, MIX_ROWS, COUT), BF16),
             pltpu.VMEM((2, y_count, MIX_ROWS, COUT), BF16),
             pltpu.VMEM((2, y_count, MIX_ROWS, COUT), BF16),
@@ -707,12 +709,12 @@
             pltpu.VMEM((far_count, MIX_ROWS, COUT), BF16),
             pltpu.VMEM((near_count, MIX_ROWS, COUT), BF16),
             pltpu.VMEM((2, MIX_ROWS, COUT), F32),
-            pltpu.VMEM((2, far_count, 16, SPAN), BF16),
-            pltpu.VMEM((2, 2 * near_count, 16, SPAN), BF16),
-            pltpu.VMEM((2, 2, 2, 16, SPAN), F32),
+            pltpu.VMEM((len(UP), far_count, 16, SPAN), BF16),
+            pltpu.VMEM((len(UP), 2 * near_count, 16, SPAN), BF16),
+            pltpu.VMEM((len(UP), 2, 2, 16, SPAN), F32),
             dma((2, PARTS)),
-            dma((4, 2, 2)),
-            dma((2, 2)),
+            dma((4, len(UP), 2)),
+            dma((2, len(UP))),
             dma((2, PARTS)),
             dma((2, PARTS)),
             dma((2, PARTS)),

time: 52.4 us -> 52.6 us (level)
  no operation moved by 1% of the time
where the time goes in v9:
time: 52.6 us; the launch traced here: 52.4 us
  Pallas kernels  51.8 us (98%)
  between operations  0.64 us (1%)
    pallas_call x1, Pallas kernels, shards(): pl.pallas_call(functools.partial(section_kernel, lat_count, lon_count, 1....  51 us

profile of v9, /device:TPU:1, one launch (start us, length us, event | category | flops | bytes accessed | tf_op | source)
XLA Modules:
  0.0 52.4 jit_solution(10548356123002552084)
XLA Ops:
  0.6 51.0 %shard_map.93 = (bf16[512,128]{1,0:T(8,128)(2,1)S(1)}, f32[128,256]{1,0:T(8,128)S(1)}, f32[4,4,16,128]{3,2,1,0:T(8,128)S(1)}, f32[9,8,128]{2,1,0:T(8,128)S(1)}) custom-call(s32[128,256]{1,0:T(8,128)} %bitcast.13, s32[64,16]{1,0:T(8,128)} %bitcast.15, bf16[512,128]{1,0:T(8,128)(2,1)} %bitcast.14, bf16[16,256,128]{2,1,0:T(8,128)(2,1)} %bitcast.11, ...), custom_call_target="tpu_custom_call" | custom-call | tf_op jit(solution)/shard_map/pallas_call | solution.py:668
  51.6 0.8 %shard_map.94 = (bf16[512,128]{1,0:T(8,128)(2,1)}, f32[128,256]{1,0:T(8,128)}, f32[4,4,16,128]{3,2,1,0:T(8,128)}, f32[9,8,128]{2,1,0:T(8,128)}) custom-call(bf16[512,128]{1,0:T(8,128)(2,1)S(1)} %get-tuple-element.12.refs_0_, f32[128,256]{1,0:T(8,128)S(1)} %get-tuple-element.13.refs_1_, f32[4,4,16,128]{3,2,1,0:T(8,128)S(1)} %get-tuple-element.14.refs_2_, ...), custom_call_target="tpu_custom_call" | custom-call | tf_op jit(solution)/shard_map/pallas_call | solution.py:727

commit v10 on v8

--- a/solution.py
+++ b/solution.py
@@ -121,20 +121,23 @@
     ]
 
 
-def halo_place(lat, lat_count, grid, row_in, col_in, corner_in):
+def halo_place(copies, lat, lat_count, grid, row_in, col_in, corner_in):
     above = (lat > 0).astype(F32)
     below = (lat < lat_count - 1).astype(F32)
     for side, (r, keep) in enumerate(((0, above), (ROWS + 1, below))):
+        copies[side].wait_recv()
         at = r * PITCH + 1
         for i in range(TALL // 2):
             part = row_in[side, i].astype(F32) * keep
             grid[2 * i, at : at + COLS, :] = part[:COLS]
             grid[2 * i + 1, at : at + COLS, :] = part[COLS:]
     for side, c in enumerate((0, COLS + 1)):
+        copies[2 + side].wait_recv()
         for i in range(TALL):
             grid[i, pl.ds(PITCH + c, ROWS, stride=PITCH), :] = col_in[side, i].astype(F32)
     places = ((0, 0, above), (0, COLS + 1, above), (ROWS + 1, 0, below), (ROWS + 1, COLS + 1, below))
     for corner, (r, c, keep) in enumerate(places):
+        copies[4 + corner].wait_recv()
         cell = r * PITCH + c
         for i in range(TALL):
             grid[i, cell : cell + 1, :] = corner_in[corner, i : i + 1, :] * keep
@@ -356,8 +359,7 @@
     sums,
     core_in,
     x_out,
-    xa_in,
-    xb_in,
+    x_in,
     y_out,
     y_in,
     mix_sums,
@@ -437,14 +439,11 @@
         copy.start()
     for load in loads[3:]:
         load.wait()
-    for copy in halo:
-        copy.wait_recv()
-    halo_place(lat, lat_count, grid, row_in, col_in, corner_in)
+    halo_place(halo, lat, lat_count, grid, row_in, col_in, corner_in)
 
     def core_start(part):
         fetch(sums.at[1 - core, part], core_in.at[part], core_sem.at[0, part], core_sem.at[1, part], partner)
 
-    half = y_count // 2
     y_steps = sorted(range(1, y_count), key=lambda step: -min(step, y_count - step))
 
     def core_end(part):
@@ -509,38 +508,23 @@
                 mix_out[tap] = mix_final[owner, i * 8 : i * 8 + 8, :]
                 tap += 1
 
-    def x_first(part):
+    def x_start(part):
         core_end(part)
-        across = lax.rem(x + 2, 4)
-        for side, step in ((0, 1), (1, -1)):
+        for step in (2, 1, 3):
             fetch(
-                x_out.at[part, across, pl.ds(side * half, half)],
-                xa_in.at[part, side],
-                x_sem.at[0, part, side],
-                x_sem.at[1, part, side],
+                x_out.at[part, lax.rem(x + step, 4)],
+                x_in.at[part, step - 1],
+                x_sem.at[0, part],
+                x_sem.at[1, part],
                 at_x(step),
             )
 
-    def x_second(part):
-        for side, step in ((0, 1), (1, -1)):
-            await_bytes(xa_in.at[part, side], x_sem.at[1, part, side])
-            beside_x = lax.rem(x + step + 4, 4)
-            rows = pl.ds(side * half, half)
-            merged = x_out[part, beside_x, rows].astype(F32) + xa_in[part, side].astype(F32)
-            x_out[part, beside_x, rows] = merged.astype(BF16)
-            fetch(
-                x_out.at[part, beside_x],
-                xb_in.at[part, side],
-                x_sem.at[2, part, side],
-                x_sem.at[3, part, side],
-                at_x(step),
-            )
-
     def y_start(part):
-        for side in range(2):
-            await_bytes(xb_in.at[part, side], x_sem.at[3, part, side])
-        merged = x_out[part, x].astype(F32) + xb_in[part, 0].astype(F32) + xb_in[part, 1].astype(F32)
-        y_out[part] = merged.astype(BF16)
+        await_bytes(x_in.at[part], x_sem.at[1, part])
+        total = x_out[part, x].astype(F32)
+        for step in range(3):
+            total = total + x_in[part, step].astype(F32)
+        y_out[part] = total.astype(BF16)
         for step in y_steps:
             fetch(
                 y_out.at[part, lax.rem(y + step, y_count)],
@@ -601,10 +585,8 @@
     up_part_sums(grid, pre_grad, 1, sums)
     core_start(1)
     mix_first()
-    x_first(0)
-    x_first(1)
     for part in UP:
-        x_second(part)
+        x_start(part)
     for part in UP:
         y_start(part)
     mix_second()
@@ -629,9 +611,7 @@
     await_bytes(mix_near.at[pl.ds(0, near_count - 1)], near_sem.at[0, MIX])
     await_bytes(mix_final.at[0], final_sem.at[0, MIX])
     for part in UP:
-        for side in range(2):
-            await_bytes(xa_in.at[part, side], x_sem.at[0, part, side])
-            await_bytes(xb_in.at[part, side], x_sem.at[2, part, side])
+        await_bytes(x_in.at[part], x_sem.at[0, part])
         await_bytes(y_in.at[part], y_sem.at[0, part])
         await_bytes(core_in.at[part], core_sem.at[0, part])
         await_bytes(far.at[part, pl.ds(0, far_count - 1)], far_sem.at[0, part])
@@ -694,8 +674,7 @@
             pltpu.VMEM((2, 2, 2, CIN, SPAN), BF16),
             pltpu.VMEM((2, 2, CIN, SPAN), BF16),
             pltpu.VMEM((2, 4, y_count, 16, SPAN), BF16),
-            pltpu.VMEM((2, 2, y_count // 2, 16, SPAN), BF16),
-            pltpu.VMEM((2, 2, y_count, 16, SPAN), BF16),
+            pltpu.VMEM((2, 3, y_count, 16, SPAN), BF16),
             pltpu.VMEM((2, y_count, 16, SPAN), BF16),
             pltpu.VMEM((2, y_count - 1, 16, SPAN), BF16),
             pltpu.VMEM((2, 2, y_count, MIX_ROWS, COUT), BF16),
@@ -711,7 +690,7 @@
             pltpu.VMEM((2, 2 * near_count, 16, SPAN), BF16),
             pltpu.VMEM((2, 2, 2, 16, SPAN), F32),
             dma((2, PARTS)),
-            dma((4, 2, 2)),
+            dma((2, 2)),
             dma((2, 2)),
             dma((2, PARTS)),
             dma((2, PARTS)),

time: 52.4 us -> 52.4 us (level)
  no operation moved by 1% of the time
where the time goes in v10:
time: 52.4 us; the launch traced here: 52.3 us
  Pallas kernels  51.6 us (98%)
  between operations  0.64 us (1%)
    pallas_call x1, Pallas kernels, shards(): pl.pallas_call(functools.partial(section_kernel, lat_count, lon_count, 1....  50.9 us

profile of v10, /device:TPU:1, one launch (start us, length us, event | category | flops | bytes accessed | tf_op | source)
XLA Modules:
  0.0 52.3 jit_solution(12761017216503422917)
XLA Ops:
  0.6 50.9 %shard_map.93 = (bf16[512,128]{1,0:T(8,128)(2,1)S(1)}, f32[128,256]{1,0:T(8,128)S(1)}, f32[4,4,16,128]{3,2,1,0:T(8,128)S(1)}, f32[9,8,128]{2,1,0:T(8,128)S(1)}) custom-call(s32[128,256]{1,0:T(8,128)} %bitcast.13, s32[64,16]{1,0:T(8,128)} %bitcast.15, bf16[512,128]{1,0:T(8,128)(2,1)} %bitcast.14, bf16[16,256,128]{2,1,0:T(8,128)(2,1)} %bitcast.11, ...), custom_call_target="tpu_custom_call" | custom-call | tf_op jit(solution)/shard_map/pallas_call | solution.py:646
  51.5 0.8 %shard_map.94 = (bf16[512,128]{1,0:T(8,128)(2,1)}, f32[128,256]{1,0:T(8,128)}, f32[4,4,16,128]{3,2,1,0:T(8,128)}, f32[9,8,128]{2,1,0:T(8,128)}) custom-call(bf16[512,128]{1,0:T(8,128)(2,1)S(1)} %get-tuple-element.12.refs_0_, f32[128,256]{1,0:T(8,128)S(1)} %get-tuple-element.13.refs_1_, f32[4,4,16,128]{3,2,1,0:T(8,128)S(1)} %get-tuple-element.14.refs_2_, ...), custom_call_target="tpu_custom_call" | custom-call | tf_op jit(solution)/shard_map/pallas_call | solution.py:704

commit v11 on v10

--- a/solution.py
+++ b/solution.py
@@ -235,13 +235,9 @@
         mix_sums[core] = jnp.concatenate(rows, axis=1).astype(BF16).reshape(mix_sums.shape[1:])
 
 
-def backward_part(grid, mix_kernel, slope, outside, pre_grad):
-    backward = jnp.concatenate([mix_kernel[i] for i in range(9)], axis=1)
-    act_grad = lax.dot_general(
-        patches(positions(grid, OUTER, 2), True),
-        backward,
-        (((1,), (1,)), ((), ())),
-        preferred_element_type=F32,
+def backward_part(grid, back_mix, slope, outside, pre_grad):
+    act_grad = jnp.dot(
+        patches(positions(grid, OUTER, 2), True), back_mix[...], preferred_element_type=F32
     )
     graded = (beside(act_grad, OUTER) * slope).astype(BF16).astype(F32)
     keep_wide(pre_grad, jnp.where(outside, 0.0, graded))
@@ -341,6 +337,7 @@
     bias,
     mix_kernel,
     load_sem,
+    back_mix,
     grid,
     own,
     cot_wide,
@@ -424,10 +421,12 @@
     near_all = sorted({step % z_count for base in near_steps for step in (base, -base)})
     greeted += [at_z(step, x_hi) for step in far_all + near_all]
     greeted += [at_z(step, 1 - x_hi) for step in [0] + near_all]
-    for to in greeted:
+    for to in greeted[:8]:
         pl.semaphore_signal(barrier, inc=1, device_id=to, device_id_type=MESH)
     for load in loads:
         load.start()
+    for to in greeted[8:]:
+        pl.semaphore_signal(barrier, inc=1, device_id=to, device_id_type=MESH)
     for load in loads[:3]:
         load.wait()
     halo_fill(codes, exps, cot, grid, own, cot_wide, row_out, col_out, corner_out)
@@ -439,6 +438,8 @@
         copy.start()
     for load in loads[3:]:
         load.wait()
+    for i in range(9):
+        back_mix[i * COUT : (i + 1) * COUT, :] = mix_kernel[i].astype(F32).T.astype(BF16)
     halo_place(halo, lat, lat_count, grid, row_in, col_in, corner_in)
 
     def core_start(part):
@@ -579,7 +580,7 @@
     act_patches = patches(positions(act, INNER, 0), False)
     mix_part_sums(grid, act_patches, mix_sums)
     fetch(mix_sums.at[1 - core], mix_core_in, core_sem.at[0, MIX], core_sem.at[1, MIX], partner)
-    backward_part(grid, mix_kernel, slope, outside, pre_grad)
+    backward_part(grid, back_mix, slope, outside, pre_grad)
     up_part_sums(grid, pre_grad, 0, sums)
     core_start(0)
     up_part_sums(grid, pre_grad, 1, sums)
@@ -656,6 +657,7 @@
         scratch_shapes=[pltpu.VMEM(operand.shape, operand.dtype) for operand in operands]
         + [
             dma((6,)),
+            pltpu.VMEM((9 * COUT, COUT), BF16),
             pltpu.VMEM((TALL, FLAT, COUT), F32),
             pltpu.VMEM((TALL, CELLS, COUT), F32),
             pltpu.VMEM((4 * CELLS, COUT), F32),

time: 52.4 us -> 52.4 us (level)
  no operation moved by 1% of the time
where the time goes in v11:
time: 52.4 us; the launch traced here: 52.3 us
  Pallas kernels  51.6 us (98%)
  between operations  0.64 us (1%)
    pallas_call x1, Pallas kernels, shards(): pl.pallas_call(functools.partial(section_kernel, lat_count, lon_count, 1....  50.9 us

profile of v11, /device:TPU:1, one launch (start us, length us, event | category | flops | bytes accessed | tf_op | source)
XLA Modules:
  0.0 52.3 jit_solution(5195703737231981769)
XLA Ops:
  0.6 50.9 %shard_map.93 = (bf16[512,128]{1,0:T(8,128)(2,1)S(1)}, f32[128,256]{1,0:T(8,128)S(1)}, f32[4,4,16,128]{3,2,1,0:T(8,128)S(1)}, f32[9,8,128]{2,1,0:T(8,128)S(1)}) custom-call(s32[128,256]{1,0:T(8,128)} %bitcast.13, s32[64,16]{1,0:T(8,128)} %bitcast.15, bf16[512,128]{1,0:T(8,128)(2,1)} %bitcast.14, bf16[16,256,128]{2,1,0:T(8,128)(2,1)} %bitcast.11, ...), custom_call_target="tpu_custom_call" | custom-call | tf_op jit(solution)/shard_map/pallas_call | solution.py:647
  51.5 0.8 %shard_map.94 = (bf16[512,128]{1,0:T(8,128)(2,1)}, f32[128,256]{1,0:T(8,128)}, f32[4,4,16,128]{3,2,1,0:T(8,128)}, f32[9,8,128]{2,1,0:T(8,128)}) custom-call(bf16[512,128]{1,0:T(8,128)(2,1)S(1)} %get-tuple-element.12.refs_0_, f32[128,256]{1,0:T(8,128)S(1)} %get-tuple-element.13.refs_1_, f32[4,4,16,128]{3,2,1,0:T(8,128)S(1)} %get-tuple-element.14.refs_2_, ...), custom_call_target="tpu_custom_call" | custom-call | tf_op jit(solution)/shard_map/pallas_call | solution.py:706

commit v12 on v11

--- a/solution.py
+++ b/solution.py
@@ -585,9 +585,9 @@
     core_start(0)
     up_part_sums(grid, pre_grad, 1, sums)
     core_start(1)
-    mix_first()
     for part in UP:
         x_start(part)
+    mix_first()
     for part in UP:
         y_start(part)
     mix_second()

time: 52.4 us -> 52.4 us (level)
  no operation moved by 1% of the time
where the time goes in v12:
time: 52.4 us; the launch traced here: 52.2 us
  Pallas kernels  51.6 us (98%)
  between operations  0.64 us (1%)
    pallas_call x1, Pallas kernels, shards(): pl.pallas_call(functools.partial(section_kernel, lat_count, lon_count, 1....  50.8 us

profile of v12, /device:TPU:1, one launch (start us, length us, event | category | flops | bytes accessed | tf_op | source)
XLA Modules:
  0.0 52.2 jit_solution(15476552835417676994)
XLA Ops:
  0.6 50.8 %shard_map.93 = (bf16[512,128]{1,0:T(8,128)(2,1)S(1)}, f32[128,256]{1,0:T(8,128)S(1)}, f32[4,4,16,128]{3,2,1,0:T(8,128)S(1)}, f32[9,8,128]{2,1,0:T(8,128)S(1)}) custom-call(s32[128,256]{1,0:T(8,128)} %bitcast.13, s32[64,16]{1,0:T(8,128)} %bitcast.15, bf16[512,128]{1,0:T(8,128)(2,1)} %bitcast.14, bf16[16,256,128]{2,1,0:T(8,128)(2,1)} %bitcast.11, ...), custom_call_target="tpu_custom_call" | custom-call | tf_op jit(solution)/shard_map/pallas_call | solution.py:647
  51.4 0.8 %shard_map.94 = (bf16[512,128]{1,0:T(8,128)(2,1)}, f32[128,256]{1,0:T(8,128)}, f32[4,4,16,128]{3,2,1,0:T(8,128)}, f32[9,8,128]{2,1,0:T(8,128)}) custom-call(bf16[512,128]{1,0:T(8,128)(2,1)S(1)} %get-tuple-element.12.refs_0_, f32[128,256]{1,0:T(8,128)S(1)} %get-tuple-element.13.refs_1_, f32[4,4,16,128]{3,2,1,0:T(8,128)S(1)} %get-tuple-element.14.refs_2_, ...), custom_call_target="tpu_custom_call" | custom-call | tf_op jit(solution)/shard_map/pallas_call | solution.py:706
